TPU v7x, 128 devices: a whole 4x4x4 slice. The times are simulated.
128 devices in a mesh: lon: 16 (over z_hi, x, core), lat: 8 (over y, z_lo).
Axes of the slice: x: 4, y: 4, z: 4 (z_hi: 2, z_lo: 2; z = z_hi * 2 + z_lo), core: 2. Of those that a mesh axis runs over, the one named last changes fastest.
Arguments:
- weather: bfloat16 [2, 16, 2048, 512], P(None, 'lat', 'lon'), may hold values from -4 to 4
- windows: int32 [16], P('lat'), may hold values from 0 to 8, as said below
- window_table: int32 [16, 16], P('lat'), may hold values 0 or 1
- lon_gain: float32 [512], replicated, may hold values from 0.5 to 6, as said below
- lon_qkv: bfloat16 [512, 1536], replicated, may hold values from -0.25 to 0.25
- lon_out: bfloat16 [512, 512], replicated, may hold values from -1 to 1
- mer_gain: float32 [512], replicated, may hold values from 0.5 to 6, as said below
- mer_qkv: bfloat16 [512, 1536], replicated, may hold values from -0.25 to 0.25
- mer_out: bfloat16 [512, 512], replicated, may hold values from -0.5 to 0.5
- slopes: float32 [8], replicated, may hold values from 0.05 to 0.5
- mlp_gain: float32 [512], replicated, may hold values from 0.5 to 6, as said below
- mlp_in: bfloat16 [512, 2048], replicated, may hold values from -0.25 to 0.25
- mlp_out: bfloat16 [2048, 512], replicated, may hold values from -0.125 to 0.125
Outputs:
- updated: bfloat16 [2, 16, 2048, 512], P(None, 'lat', 'lon')
Inputs may be any that keep to these rules, and one draw needn't show every extreme that they name: Latitude-dependent: rows nearest the poles have the widest windows, 8 blocks, rows near the equator narrow ones. `lon_gain`: Positive. `mer_gain`: Positive. `mlp_gain`: Positive.
All inputs are finite; a program needn't handle non-finite values. No bound on the sum of `window_table` on one device may be relied on, other than what follows from the above.
Results may differ from a plain program's by a relative error of at most 0.027.
The roundings to bfloat16 on the way count: a program that leaves them out, or rounds other values in their place, can miss the bound.
Values may be sent and summed in bfloat16 or wider, within the bound.
A program may use at most 128 MiB of HBM per device.

v0:
```python
import math

import jax
import jax.numpy as jnp
from jax import lax
from jax.sharding import PartitionSpec as P

HEADS = 8


masked_score = -1e30
norm_eps = 1e-06


def from_behind(value, axis, by):
    devices = lax.axis_size(axis)
    return lax.ppermute(value, axis, [(i, (i + by) % devices) for i in range(devices)])


def rms_scale(values_in, gain_row):
    widened = values_in.astype(jnp.float32)
    inverse = lax.rsqrt(jnp.mean(widened * widened, axis=-1, keepdims=True) + norm_eps)
    return (widened * inverse * gain_row).astype(jnp.bfloat16)


def project(values_in, weight):
    flattened = values_in.reshape(-1, values_in.shape[-1])
    product = jnp.dot(flattened, weight, preferred_element_type=jnp.float32)
    return product.reshape(values_in.shape[:-1] + (weight.shape[1],))


def allowed_blocks(windows, window_table, query_block, cycle_blocks):
    key_block = jnp.arange(cycle_blocks, dtype=jnp.int32)
    offset = (key_block - query_block) % cycle_blocks
    reach_blocks = jnp.minimum(offset, cycle_blocks - offset)
    rotate = (key_block[:, None] == offset[None, :]).astype(jnp.float32)
    picked = jnp.dot(window_table.astype(jnp.float32), rotate)
    allowed = (reach_blocks[None, :] <= windows[:, None]) & (
        (offset[None, :] == 0) | (picked > 0.5)
    )
    return allowed.astype(jnp.float32)


def online_update(running, scores, visible, values_part, pattern):
    peak_old, total_old, accum_old = running
    hidden_scores = jnp.where(visible, scores, masked_score)
    peak_new = jnp.maximum(peak_old, jnp.max(hidden_scores, axis=-1))
    factor = jnp.exp(peak_old - peak_new)
    weights = jnp.where(visible, jnp.exp(scores - peak_new[..., None]), 0.0)
    total_new = total_old * factor + jnp.sum(weights, axis=-1)
    mixed = jnp.einsum(
        pattern, weights.astype(jnp.bfloat16), values_part, preferred_element_type=jnp.float32
    )
    return (peak_new, total_new, accum_old * factor[..., None] + mixed)


def lon_cycle(qkv_lon, allowed, cycle_blocks):
    samples, lat_rows, block_cells, triple = qkv_lon.shape
    channels = triple // 3
    head_dim = channels // HEADS
    score_scale = 1.0 / math.sqrt(head_dim)
    queries = qkv_lon[..., :channels].reshape(samples, lat_rows, block_cells, HEADS, head_dim)
    keys_local = qkv_lon[..., channels : 2 * channels]
    values_local = qkv_lon[..., 2 * channels :]
    start_carry = (
        jnp.full((samples, lat_rows, HEADS, block_cells), masked_score, jnp.float32),
        jnp.zeros((samples, lat_rows, HEADS, block_cells), jnp.float32),
        jnp.zeros((samples, lat_rows, HEADS, block_cells, head_dim), jnp.float32),
    )
    keys_all = lax.all_gather(keys_local, "lon", axis=2, tiled=True)
    values_all = lax.all_gather(values_local, "lon", axis=2, tiled=True)
    length = keys_all.shape[2]

    def one_block(running, block_index):
        first_cell = block_index * block_cells
        keys_part = lax.dynamic_slice_in_dim(keys_all, first_cell, block_cells, 2)
        keys_part = keys_part.reshape(samples, lat_rows, block_cells, HEADS, head_dim)
        values_part = lax.dynamic_slice_in_dim(values_all, first_cell, block_cells, 2)
        values_part = values_part.reshape(samples, lat_rows, block_cells, HEADS, head_dim)
        cell_index = first_cell + jnp.arange(block_cells, dtype=jnp.int32)
        onehot = (
            jnp.arange(cycle_blocks, dtype=jnp.int32)[:, None]
            == (cell_index // block_cells)[None, :]
        ).astype(jnp.float32)
        visible = jnp.dot(allowed, onehot) > 0.5
        scores = (
            jnp.einsum("btqhd,btkhd->bthqk", queries, keys_part, preferred_element_type=jnp.float32)
            * score_scale
        )
        updated_state = online_update(
            running, scores, visible[None, :, None, None, :], values_part, "bthqk,btkhd->bthqd"
        )
        return (updated_state, None)

    carry_out, _ = lax.scan(
        one_block, start_carry, jnp.arange(length // block_cells, dtype=jnp.int32)
    )
    _, total_all, accum_all = carry_out
    result = accum_all / total_all[..., None]
    result = jnp.transpose(result, (0, 1, 3, 2, 4)).reshape(
        samples, lat_rows, block_cells, channels
    )
    return result.astype(jnp.bfloat16)


def band_distance(own_rows, other_rows, circle_rows):
    same_half = jnp.abs(own_rows[:, None] - other_rows[None, :])
    crossed = jnp.minimum(
        circle_rows - 1 - own_rows[:, None] - other_rows[None, :],
        own_rows[:, None] + other_rows[None, :] + 1,
    )
    return (same_half.astype(jnp.float32), crossed.astype(jnp.float32))


def mer_gather(qkv_mer, partner, slopes, band_index, band_count):
    samples, lat_rows, block_cells, triple = qkv_mer.shape
    channels = triple // 3
    head_dim = channels // HEADS
    score_scale = 1.0 / math.sqrt(head_dim)
    circle_rows = 2 * lat_rows * band_count
    own_rows = band_index * lat_rows + jnp.arange(lat_rows, dtype=jnp.int32)
    queries = qkv_mer[..., :channels].reshape(samples, lat_rows, block_cells, HEADS, head_dim)
    own_local = qkv_mer[..., channels:]
    start_carry = (
        jnp.full((samples, block_cells, HEADS, lat_rows), masked_score, jnp.float32),
        jnp.zeros((samples, block_cells, HEADS, lat_rows), jnp.float32),
        jnp.zeros((samples, block_cells, HEADS, lat_rows, head_dim), jnp.float32),
    )
    own_part = lax.all_gather(own_local, "lat", axis=1, tiled=True)
    partner_part = lax.all_gather(partner, "lat", axis=1, tiled=True)
    length = own_part.shape[1]
    other_rows = jnp.arange(length, dtype=jnp.int32)
    near_dist, far_dist = band_distance(own_rows, other_rows, circle_rows)
    running = start_carry
    for member, distance in ((own_part, near_dist), (partner_part, far_dist)):
        keys_part = member[..., :channels].reshape(samples, length, block_cells, HEADS, head_dim)
        values_part = member[..., channels:].reshape(samples, length, block_cells, HEADS, head_dim)
        scores = (
            jnp.einsum("btchd,bschd->bchts", queries, keys_part, preferred_element_type=jnp.float32)
            * score_scale
        )
        scores = scores - slopes[None, None, :, None, None] * distance[None, None, None]
        running = online_update(running, scores, True, values_part, "bchts,bschd->bchtd")
    _, total_all, accum_all = running
    result = accum_all / total_all[..., None]
    result = jnp.transpose(result, (0, 3, 1, 2, 4)).reshape(
        samples, lat_rows, block_cells, channels
    )
    return result.astype(jnp.bfloat16)


def per_device(
    weather,
    windows,
    window_table,
    lon_gain,
    lon_qkv,
    lon_out,
    mer_gain,
    mer_qkv,
    mer_out,
    slopes,
    mlp_gain,
    mlp_in,
    mlp_out,
):
    cycle_blocks = lax.axis_size("lon")
    band_count = lax.axis_size("lat")
    channels = weather.shape[-1]
    normed_lon = rms_scale(weather, lon_gain)
    qkv_lon = project(normed_lon, lon_qkv).astype(jnp.bfloat16)
    allowed = allowed_blocks(windows, window_table, lax.axis_index("lon"), cycle_blocks)
    attn_lon = lon_cycle(qkv_lon, allowed, cycle_blocks)
    mixed_lon = (weather.astype(jnp.float32) + project(attn_lon, lon_out)).astype(jnp.bfloat16)
    normed_mer = rms_scale(mixed_lon, mer_gain)
    qkv_mer = project(normed_mer, mer_qkv).astype(jnp.bfloat16)
    partner = from_behind(qkv_mer[..., channels:], "lon", cycle_blocks // 2)
    attn_mer = mer_gather(qkv_mer, partner, slopes, lax.axis_index("lat"), band_count)
    mixed_mer = (mixed_lon.astype(jnp.float32) + project(attn_mer, mer_out)).astype(jnp.bfloat16)
    normed_mlp = rms_scale(mixed_mer, mlp_gain)
    hidden = jax.nn.gelu(project(normed_mlp, mlp_in)).astype(jnp.bfloat16)
    return (mixed_mer.astype(jnp.float32) + project(hidden, mlp_out)).astype(jnp.bfloat16)


def solution(mesh):
    return jax.shard_map(
        per_device,
        mesh=mesh,
        in_specs=(
            P(None, "lat", "lon", None),
            P("lat"),
            P("lat", None),
            P(),
            P(),
            P(),
            P(),
            P(),
            P(),
            P(),
            P(),
            P(),
            P(),
        ),
        out_specs=P(None, "lat", "lon", None),
        check_vma=False,
    )
```

profile of v0, /device:TPU:1, one launch (start us, length us, event | category | flops | bytes accessed | tf_op | source)
XLA Modules:
  0.0 841.2 jit_solution(7167920793766050382)
XLA Ops:
  13.7 74.5 %all-gather.5.cloned.1.call-done = bf16[2,2,2048,512]{3,2,1,0:T(8,128)(2,1)} async-done(((bf16[2,2,128,512]{3,2,1,0:T(8,128)(2,1)}), bf16[2,2,2048,512]{3,2,1,0:T(8,128)(2,1)}) %all-gather.5.cloned.1.call-update) | async-done | bytes 8388624 | tf_op jit(solution)/shard_map/all_gather | solution.py:70
  88.2 72.9 %all-gather.7.cloned.1.call-done = bf16[2,2,2048,512]{3,2,1,0:T(8,128)(2,1)} async-done(((bf16[2,2,128,512]{3,2,1,0:T(8,128)(2,1)}), bf16[2,2,2048,512]{3,2,1,0:T(8,128)(2,1)}) %all-gather.7.cloned.1.call-update) | async-done | bytes 8388624 | tf_op jit(solution)/shard_map/all_gather | solution.py:71
  161.2 200.8 %while.17 = (s32[]{:T(128)}, f32[2,2,8,128]{3,2,1,0:T(8,128)S(1)}, f32[2,2,8,128]{3,2,1,0:T(8,128)S(1)}, f32[2,2,8,128,64]{3,4,2,1,0:T(8,128)}, s32[16]{0:T(128)...) while((s32[]{:T(128)}, f32[2,2,8,128]{3,2,1,0:T(8,128)S(1)}, ...), condition=%wide.region_4.5_spmd.clone, body=%wide.region_1.4_spmd.clone.sunk | while | flops 140804352 | bytes 14420235 | solution.py:95
  170.4 3.1 convolution_add_fusion.2
  177.2 3.1 select_reduce_fusion.2
  182.7 3.4 convolution_add_fusion.2
  189.7 3.1 select_reduce_fusion.2
  195.2 3.4 convolution_add_fusion.2
  202.3 3.1 select_reduce_fusion.2
  207.8 3.4 convolution_add_fusion.2
  220.4 3.4 convolution_add_fusion.2
  227.4 3.1 select_reduce_fusion.2
  232.9 3.4 convolution_add_fusion.2
  245.5 3.4 convolution_add_fusion.2
  252.6 3.1 select_reduce_fusion.2
  258.1 3.4 convolution_add_fusion.2
  270.6 3.4 convolution_add_fusion.2
  277.7 3.1 select_reduce_fusion.2
  283.2 3.4 convolution_add_fusion.2
  295.8 3.4 convolution_add_fusion.2
  302.9 3.1 select_reduce_fusion.2
  308.4 3.4 convolution_add_fusion.2
  320.9 3.4 convolution_add_fusion.2
  328.0 3.1 select_reduce_fusion.2
  333.5 3.4 convolution_add_fusion.2
  346.1 3.4 convolution_add_fusion.2
  353.1 3.1 select_reduce_fusion.2
  358.6 3.4 convolution_add_fusion.2
  369.1 68.1 %collective-permute-done = bf16[2,2,128,1024]{3,2,1,0:T(8,128)(2,1)} collective-permute-done((bf16[2,2,128,1024]{3,2,1,0:T(8,128)(2,1)}, bf16[2,2,128,1024]{3,2,1,0:T(8,128)(2,1)}, u32[]{:S(2)}, u32[]{:S(2)}) %collective-permute-start) | collective-permute-done | bytes 1048608 | tf_op jit(solution)/shard_map/ppermute | solution.py:17
  439.7 112.4 %all-gather.9.cloned.1.call-done = bf16[2,16,128,1024]{3,2,1,0:T(8,128)(2,1)} async-done(((bf16[2,2,128,1024]{3,2,1,0:T(8,128)(2,1)}), bf16[2,16,128,1024]{3,2,1,0:T(8,128)(2,1)}) %all-gather.9.cloned.1.call-update) | async-done | bytes 8388624 | tf_op jit(solution)/shard_map/all_gather | solution.py:129
  552.1 5.9 fusion.84
  557.9 6.3 copy.72
  564.2 13.1 %copy.74 = bf16[2,16,128,8,64]{4,1,3,2,0:T(8,128)(2,1)} copy(bf16[2,16,128,8,64]{2,4,3,1,0:T(8,128)(2,1)} %bitcast.135) | data formatting | bytes 8388608 | tf_op jit(solution)/shard_map/reshape | solution.py:136
  577.3 10.2 %fusion.87 = (f32[2,128,8,2]{3,2,1,0:T(8,128)}, f32[2,128,8,2,16]{4,3,2,1,0:T(2,128)}) fusion(f32[8,2,16]{2,1,0:T(2,128)S(1)} %get-tuple-element.225, bf16[2,2,128,8,64]{4,1,3,2,0:T(2,128)(2,1)S(1)} %copy-done.4, bf16[2,16,128,8,64]{4,1,3,2,0:T(8,128)(2,1)} %copy.74), kind=kOutput, calls=%fused_computation.129 | convolution fusion | flops 8581120 | bytes 4998144 | tf_op jit(solution)/shard_map/btchd,bschd->bchts/dot_general | solution.py:139
  589.1 6.3 copy.78
  595.4 13.0 %copy.79 = bf16[2,16,128,8,64]{4,1,3,2,0:T(8,128)(2,1)} copy(bf16[2,16,128,8,64]{2,4,3,1,0:T(8,128)(2,1)} %bitcast.136) | data formatting | bytes 8388608 | tf_op jit(solution)/shard_map/reshape | solution.py:137
  608.4 117.2 %all-gather.11.cloned.1.call-done = bf16[2,16,128,1024]{3,2,1,0:T(8,128)(2,1)} async-done(((bf16[2,2,128,1024]{3,2,1,0:T(8,128)(2,1)}), bf16[2,16,128,1024]{3,2,1,0:T(8,128)(2,1)}) %all-gather.11.cloned.1.call-update) | async-done | bytes 8388624 | tf_op jit(solution)/shard_map/all_gather | solution.py:130
  725.6 5.9 fusion.83
  731.5 6.3 copy.80
  737.8 13.0 %copy.82 = bf16[2,16,128,8,64]{4,1,3,2,0:T(8,128)(2,1)} copy(bf16[2,16,128,8,64]{2,4,3,1,0:T(8,128)(2,1)} %bitcast.137) | data formatting | bytes 8388608 | tf_op jit(solution)/shard_map/reshape | solution.py:136
  750.8 10.3 %fusion.86 = (f32[2,128,8,2]{3,2,1,0:T(8,128)}, f32[2,128,8,2,16]{4,3,2,1,0:T(2,128)}) fusion(f32[8,2,16]{2,1,0:T(2,128)S(1)} %get-tuple-element.224, bf16[2,2,128,8,64]{4,1,3,2,0:T(2,128)(2,1)S(1)} %copy-done.4, bf16[2,16,128,8,64]{4,1,3,2,0:T(8,128)(2,1)} %copy.82), kind=kOutput, calls=%fused_computation.128 | convolution fusion | flops 8581120 | bytes 4998144 | tf_op jit(solution)/shard_map/btchd,bschd->bchts/dot_general | solution.py:139
  763.0 8.0 fusion.38
  773.0 7.7 fusion.40
  786.4 6.9 fusion.43
  793.2 6.3 copy.87
  799.5 13.0 %copy.88 = bf16[2,16,128,8,64]{4,1,3,2,0:T(8,128)(2,1)} copy(bf16[2,16,128,8,64]{2,4,3,1,0:T(8,128)(2,1)} %bitcast.138) | data formatting | bytes 8388608 | tf_op jit(solution)/shard_map/reshape | solution.py:137
  812.5 12.8 %fusion.22 = bf16[2,2,128,8,64]{4,1,3,2,0:T(2,128)(2,1)} fusion(f32[2,128,8,2,64]{4,3,2,1,0:T(2,128)} %fusion.43, bf16[2,16,128,8,64]{4,1,3,2,0:T(8,128)(2,1)} %copy.88, f32[2,128,8,2,16]{4,3,2,1,0:T(2,128)} %get-tuple-element.231, f32[2,2,128,8]{1,3,2,0:T(8,128)} %copy.91, f32[2,128,8,2]{3,2,1,0:T(8,128)S(1)} %copy.86, f32[2,2,128,8]{1,3,2,0:T(8,128)} %copy.84, ...), kind=kOutput, calls=%fused_computation.48 | convolution fusion | flops 9830400 | bytes 6094848 | tf_op jit(solution)/shard_map/bchts,bschd->bchtd/dot_general | solution.py:51
  829.6 5.1 fusion.29
  (236 shorter events, 140.1 us)
Async XLA Ops:
  6.5 823.0 %copy-start = (bf16[2048,512]{1,0:T(8,128)(2,1)S(1)}, bf16[2048,512]{1,0:T(8,128)(2,1)}, u32[]{:S(2)}) copy-start(bf16[2048,512]{1,0:T(8,128)(2,1)} %param.27) | copy-start | bytes 6291460
  6.5 81.7 %all-gather.5.cloned.1.call-start = ((), (), s32[]{:S(2)}) async-start(), calls=%async_computation | async-start | bytes 8912896 | tf_op jit(solution)/shard_map/all_gather | solution.py:70
  10.5 3.0 copy-start.9
  10.6 3.0 copy-start.10
  11.7 149.5 %all-gather.7.cloned.1.call-start = ((), (), s32[]{:S(2)}) async-start(), calls=%async_computation.1 | async-start | bytes 8912896 | tf_op jit(solution)/shard_map/all_gather | solution.py:71
  12.5 539.6 %all-gather.9.cloned.1.call-start = ((), (), s32[]{:S(2)}) async-start(), calls=%async_computation.2 | async-start | bytes 9437184 | tf_op jit(solution)/shard_map/all_gather | solution.py:129
  362.0 3.3 copy-start.6
  362.0 3.3 copy-start.7
  365.3 1.1 copy-start.2
  366.4 1.2 copy-start.3
  367.5 69.7 %copy-start.5 = (f32[8]{0:T(128)S(1)}, f32[8]{0:T(128)}, u32[]{:S(2)}) copy-start(f32[8]{0:T(128)} %param.24) | copy-start | bytes 100
  368.6 68.7 %slice-start = ((bf16[2,2,128,1536]{3,2,1,0:T(8,128)(2,1)}), bf16[2,2,128,512]{3,2,1,0:T(8,128)(2,1)S(1)}, s32[]{:S(2)}) async-start(bf16[2,2,128,1536]{3,2,1,0:T(8,128)(2,1)} %copy-done.3), calls=%async_computation.4 | async-start | bytes 1048576 | tf_op jit(solution)/shard_map/slice | solution.py:122
  368.7 356.9 %all-gather.11.cloned.1.call-start = ((), (), s32[]{:S(2)}) async-start(), calls=%async_computation.3 | async-start | bytes 9437184 | tf_op jit(solution)/shard_map/all_gather | solution.py:130
  368.7 68.4 %collective-permute-start = (bf16[2,2,128,1024]{3,2,1,0:T(8,128)(2,1)}, bf16[2,2,128,1024]{3,2,1,0:T(8,128)(2,1)}, u32[]{:S(2)}, u32[]{:S(2)}) collective-permute-start(bf16[2,2,128,1024]{3,2,1,0:T(8,128)(2,1)} %slice.41), channel_id=1, source_target_pairs={{0,64},{8,72},{16,80},{24,88},{32,96},{40,104},{48,112},{56,120},{... | collective-permute-start | bytes 3145736 | tf_op jit(solution)/shard_map/ppermute | solution.py:17
  564.2 13.1 %copy-start.4 = (bf16[2,2,128,8,64]{4,1,3,2,0:T(2,128)(2,1)S(1)}, bf16[2,2,128,8,64]{4,1,3,2,0:T(2,128)(2,1)}, u32[]{:S(2)}) copy-start(bf16[2,2,128,8,64]{4,1,3,2,0:T(2,128)(2,1)} %copy.73) | copy-start | bytes 1572868
  763.0 8.0 copy-start.1
  825.3 4.3 copy-start.8
Sparse Core Ops, SparseCore 0:
  11.8 76.3 all-gather.4
  90.7 70.4 all-gather.6
  368.8 183.2 all-gather.8
  553.6 171.9 all-gather.10
where the time goes:
time: 848 us; the launch traced here: 841 us
  waiting for transfers between devices  446 us (53%)
  local copies, waits for them, and re-layouts  160 us (19%)
  matrix products  158 us (19%)
  other arithmetic  52.4 us (6%)
  between operations  13.4 us (2%)
  loops' own time  11 us (1%)
    all_gather x1, waiting for transfers between devices, mer_gather(): partner_part = lax.all_gather(partner, 'lat', axis=1, tiled=True)  117 us
    all_gather x1, waiting for transfers between devices, mer_gather(): own_part = lax.all_gather(own_local, 'lat', axis=1, tiled=True)  112 us
    all_gather x1, waiting for transfers between devices, lon_cycle(): keys_all = lax.all_gather(keys_local, 'lon', axis=2, tiled=True)  74.5 us
    dot_general x18, matrix products, online_update(): jnp.einsum(pattern, weights.astype(jnp.bfloat16), values_part, preferred_...  73.4 us
    all_gather x1, waiting for transfers between devices, lon_cycle(): values_all = lax.all_gather(values_local, 'lon', axis=2, tiled=True)  72.9 us
    ppermute x1, waiting for transfers between devices, from_behind(): lax.ppermute(value, axis, [(i, (i + by) % devices) for i in range(devices)])  68.1 us
    dot_general x16, matrix products, one_block(): jnp.einsum('btqhd,btkhd->bthqk', queries, keys_part, preferred_element_ty...  49.8 us
    reduce_sum x18, other arithmetic, online_update(): total_new = total_old * factor + jnp.sum(weights, axis=-1)  48.8 us
  transfers between devices with their start and end apart: 5, of which 5 were waited for; matrix products, arithmetic and copies ran while one was open for 7% of the time, Pallas kernels for 0%

commit v1 on v0

v1 whole, which is shorter than its diff:
```python
import functools

import jax
import jax.numpy as jnp
from jax import lax
from jax.experimental import pallas as pl
from jax.experimental.pallas import tpu as pltpu
from jax.sharding import PartitionSpec as P

MESH = pl.DeviceIdType.MESH
F32 = jnp.float32
BF16 = jnp.bfloat16
BLOCK = 128
CH = 512
NEG = -1e30
EPS = 1e-06


def rms(x, gain):
    inv = lax.rsqrt(jnp.mean(x * x, axis=-1, keepdims=True) + EPS)
    return (x * inv * gain).astype(BF16)


def dot(a, b):
    return jnp.dot(a, b, preferred_element_type=F32)


def dot_nt(a, b):
    return lax.dot_general(a, b, (((1,), (1,)), ((), ())), preferred_element_type=F32)


def kernel(
    weather, windows, table, lon_gain, mer_gain, mlp_gain, slopes,
    lon_qkv_h, lon_out_h, mer_qkv_h, mer_out_h, mlp_in_h, mlp_out_h,
    out,
    rowx, kt, vaug, qs, attn, mixed, merx, xg, mqkv, outs, bias, dist,
    lon_qkv, lon_out, mer_qkv, mer_out, mlp_in, mlp_out,
    w_sem, l_sem, lon_ss, lon_rs, fwd_ss, fwd_rs, mer_ss, mer_rs, out_ss, out_rs,
):
    lo, band = lax.axis_index("lon"), lax.axis_index("lat")
    zh, x, c = lo // 8, (lo // 2) % 4, lo % 2
    y, zl = band // 2, band % 2
    base, r = (x // 2) * 2, x % 2
    s = (x // 2 + zh) % 2

    def dev(zh, x, c, y, zl):
        return ((zh * 4 + x) * 2 + c, y * 2 + zl)

    loads = [
        pltpu.make_async_copy(src, dst, w_sem.at[i])
        for i, (src, dst) in enumerate(
            [(lon_qkv_h, lon_qkv), (lon_out_h, lon_out), (mer_qkv_h, mer_qkv),
             (mer_out_h, mer_out), (mlp_in_h, mlp_in), (mlp_out_h, mlp_out)]
        )
    ]
    own_copy = pltpu.make_async_copy(weather.at[s, r], rowx.at[lo], l_sem.at[0])
    own_copy.start()
    loads[0].start()

    barrier = pltpu.get_barrier_semaphore()
    peers = [dev((zh + dz) % 2, (x + dx) % 4, c, y, zl) for dz in range(2) for dx in range(4) if dz + dx]
    peers.append(dev(zh, x, 1 - c, y, zl))
    lat_steps = [(dy, dl) for dy in range(4) for dl in range(2)]
    peers += [
        dev(zh, base + (r + dr) % 2, c, (y + dy) % 4, (zl + dl) % 2)
        for dr in range(2) for dy, dl in lat_steps if dr + dy + dl
    ]
    peers += [dev(1 - zh, x, c, (y + dy) % 4, (zl + dl) % 2) for dy, dl in lat_steps if dy + dl]
    for peer in peers:
        pl.semaphore_signal(barrier, inc=1, device_id=peer, device_id_type=MESH)
    pl.semaphore_wait(barrier, len(peers))

    def lon_copy(n):
        dz, dx = n // 4, n % 4
        tz, tx = (zh + dz) % 2, (x + dx) % 4
        return pltpu.make_async_remote_copy(
            src_ref=weather.at[(tx // 2 + tz) % 2, tx % 2],
            dst_ref=rowx.at[lo],
            send_sem=lon_ss.at[n],
            recv_sem=lon_rs.at[n],
            device_id=dev(tz, tx, c, y, zl),
            device_id_type=MESH,
        )

    def piece_of(n, core):
        dz, dx = n // 4, n % 4
        return (((zh + dz) % 2) * 4 + (x + 4 - dx) % 4) * 2 + core

    def fwd_copy(n):
        piece = piece_of(n, c)
        return pltpu.make_async_remote_copy(
            src_ref=rowx.at[piece],
            dst_ref=rowx.at[piece],
            send_sem=fwd_ss.at[n],
            recv_sem=fwd_rs.at[n],
            device_id=dev(zh, x, 1 - c, y, zl),
            device_id_type=MESH,
        )

    for n in (4, 6, 5, 7, 2, 1, 3):
        lon_copy(n).start()
    for load in loads[1:]:
        load.start()

    width = windows[r]
    row8 = lax.broadcasted_iota(jnp.int32, (8, BLOCK), 0)

    @pl.loop(0, 16)
    def _(kb):
        value = jnp.zeros((8, BLOCK), F32)
        for qi in range(4):
            qb = (qi // 2) * 8 + (base + qi % 2) * 2 + c
            d = (kb - qb + 16) % 16
            seen = (jnp.minimum(d, 16 - d) <= width) & ((d == 0) | (table[r, d] == 1))
            value = jnp.where(row8 == qi, jnp.where(seen, 0.0, NEG), value)
        bias[:, pl.ds(pl.multiple_of(kb * BLOCK, BLOCK), BLOCK)] = value

    def position(i):
        row, half = i // 16, (i // 8) % 2
        return jnp.where(half == 0, row, 31 - row)

    ii = lax.broadcasted_iota(jnp.int32, (256, 256), 0)
    jj = lax.broadcasted_iota(jnp.int32, (256, 256), 1)
    apart = jnp.abs(position(ii) - position(jj))
    apart = jnp.minimum(apart, 32 - apart).astype(F32)
    dist[...] = jnp.where(ii % 8 == jj % 8, apart, -1.0)

    loads[0].wait()
    low_half = lax.broadcasted_iota(jnp.int32, (BLOCK, BLOCK), 1) < 64
    one = jnp.ones((BLOCK, BLOCK), BF16)

    def keys_values(piece):
        normed = rms(rowx[piece].astype(F32), lon_gain[...])
        cells = pl.ds(pl.multiple_of(piece * BLOCK, BLOCK), BLOCK)
        k = dot(normed, lon_qkv[:, CH : 2 * CH])
        kt[:, :, cells] = k.T.astype(BF16).reshape(4, BLOCK, BLOCK)
        v = dot(normed, lon_qkv[:, 2 * CH :]).astype(BF16)
        for hp in range(4):
            part = v[:, hp * BLOCK : (hp + 1) * BLOCK]
            vaug[2 * hp, cells, :] = jnp.where(low_half, part, one)
            vaug[2 * hp + 1, cells, :] = jnp.where(low_half, one, part)

    @pl.loop(0, 9)
    def _(n):
        @pl.when(n == 0)
        def _():
            own_copy.wait()

        @pl.when((n > 0) & (n < 8))
        def _():
            lon_copy(n).wait_recv()

        @pl.when(n < 8)
        def _():
            fwd_copy(n).start()
            keys_values(piece_of(n, c))

        @pl.when(n > 0)
        def _():
            fwd_copy(n - 1).wait_recv()
            keys_values(piece_of(n - 1, 1 - c))

    def query_block(qi):
        return (qi // 2) * 8 + (base + qi % 2) * 2 + c

    for qi in range(4):
        normed = rms(rowx[query_block(qi)].astype(F32), lon_gain[...])
        q = dot(normed, lon_qkv[:, :CH]).astype(BF16) * jnp.bfloat16(0.125)
        for hp in range(4):
            qs[hp, qi * BLOCK : (qi + 1) * BLOCK, :] = q[:, hp * BLOCK : (hp + 1) * BLOCK]

    low_256 = lax.broadcasted_iota(jnp.int32, (256, BLOCK), 1) < 64
    none = jnp.zeros((256, BLOCK), BF16)

    @pl.loop(0, 8)
    def _(step):
        hp, qt = step // 2, step % 2
        rows = pl.ds(pl.multiple_of(qt * 256, 256), 256)
        qp = qs[hp, rows, :]
        half_bias = [bias[pl.ds(qt * 2 + j, 1), :] for j in range(2)]
        res = []
        for hh in range(2):
            qm = jnp.where(low_256, qp, none) if hh == 0 else jnp.where(low_256, none, qp)
            sc = dot(qm, kt[hp])
            sc = jnp.concatenate([sc[:BLOCK] + half_bias[0], sc[BLOCK:] + half_bias[1]], axis=0)
            m = jnp.max(sc, axis=-1, keepdims=True)
            p = jnp.exp(sc - m).astype(BF16)
            o = dot(p, vaug[2 * hp + hh])
            res.append(o / pltpu.roll(o, 64, 1))
        attn[rows, pl.ds(pl.multiple_of(hp * BLOCK, BLOCK), BLOCK)] = jnp.where(
            low_256, res[0], res[1]
        ).astype(BF16)

    loads[1].wait()
    for qi in range(4):
        new = dot(attn[qi * BLOCK : (qi + 1) * BLOCK, :], lon_out[...])
        mixed[qi // 2, qi % 2] = (rowx[query_block(qi)].astype(F32) + new).astype(BF16)

    def mer_copy(dr, dy, dl):
        tr, ty, tl = (r + dr) % 2, (y + dy) % 4, (zl + dl) % 2
        n = (dr * 4 + dy) * 2 + dl
        src = mixed.at[:, tr, pl.ds(pl.multiple_of((ty * 2 + tl) * 16, 16), 16), :]
        dst = merx.at[band * 2 + r]
        if n == 0:
            return pltpu.make_async_copy(src, dst, l_sem.at[1])
        return pltpu.make_async_remote_copy(
            src_ref=src, dst_ref=dst, send_sem=mer_ss.at[n], recv_sem=mer_rs.at[n],
            device_id=dev(zh, base + tr, c, ty, tl), device_id_type=MESH,
        )

    mer_steps = [(dr, dy, dl) for dr in range(2) for dy, dl in lat_steps]
    for step in mer_steps:
        mer_copy(*step).start()
    for load in loads[2:]:
        load.wait()
    for step in mer_steps:
        if sum(step):
            mer_copy(*step).wait_recv()
        else:
            mer_copy(*step).wait()

    cells = merx[...].astype(F32).reshape(32, 2, 8, CH)
    for g in range(2):
        part = cells[:, g].reshape(256, CH)
        xg[g * 256 : (g + 1) * 256, :] = part
        qkv = dot(rms(part, mer_gain[...]), mer_qkv[...]).astype(BF16)
        for j in range(12):
            mqkv[j, g * 256 : (g + 1) * 256, :] = qkv[:, j * BLOCK : (j + 1) * BLOCK]

    ones_256 = jnp.ones((256, BLOCK), BF16)

    @pl.loop(0, 4)
    def _(hp):
        far = dist[...]
        for g in range(2):
            rows = slice(g * 256, (g + 1) * 256)
            qp = mqkv[hp, rows, :] * jnp.bfloat16(0.125)
            kp = mqkv[4 + hp, rows, :]
            vp = mqkv[8 + hp, rows, :]
            res = []
            for hh in range(2):
                qm = jnp.where(low_256, qp, none) if hh == 0 else jnp.where(low_256, none, qp)
                vm = jnp.where(low_256, vp, ones_256) if hh == 0 else jnp.where(low_256, ones_256, vp)
                sc = dot_nt(qm, kp) - far * slopes[2 * hp + hh]
                sc = jnp.where(far >= 0.0, sc, NEG)
                m = jnp.max(sc, axis=-1, keepdims=True)
                p = jnp.exp(sc - m).astype(BF16)
                o = dot(p, vm)
                res.append(o / pltpu.roll(o, 64, 1))
            attn[rows, pl.ds(pl.multiple_of(hp * BLOCK, BLOCK), BLOCK)] = jnp.where(
                low_256, res[0], res[1]
            ).astype(BF16)

    parts = []
    for g in range(2):
        rows = slice(g * 256, (g + 1) * 256)
        mm = (xg[rows, :] + dot(attn[rows, :], mer_out[...])).astype(BF16).astype(F32)
        normed = rms(mm, mlp_gain[...])
        xg[rows, :] = mm
        attn[rows, :] = normed

    @pl.loop(0, 4)
    def _(j):
        cols = pl.ds(pl.multiple_of(j * CH, CH), CH)
        hidden = jax.nn.gelu(dot(attn[...], mlp_in[:, cols])).astype(BF16)
        xg[...] += dot(hidden, mlp_out[cols, :])

    done = jnp.swapaxes(xg[...].reshape(2, 32, 8, CH), 0, 1)
    outs[...] = done.reshape(16, 2, 16, CH).astype(BF16)

    def out_copy(dz, dy, dl):
        tz, ty, tl = (zh + dz) % 2, (y + dy) % 4, (zl + dl) % 2
        n = (dz * 4 + dy) * 2 + dl
        src = outs.at[pl.ds((ty * 2 + tl) * 2, 2), tz]
        dst = out.at[s, :, pl.ds(pl.multiple_of(band * 16, 16), 16), :]
        if n == 0:
            return pltpu.make_async_copy(src, dst, l_sem.at[2])
        return pltpu.make_async_remote_copy(
            src_ref=src, dst_ref=dst, send_sem=out_ss.at[n], recv_sem=out_rs.at[n],
            device_id=dev(tz, x, c, ty, tl), device_id_type=MESH,
        )

    for step in mer_steps:
        out_copy(*step).start()
    for n in range(1, 8):
        lon_copy(n).wait_send()
    for n in range(8):
        fwd_copy(n).wait_send()
    for step in mer_steps:
        if sum(step):
            mer_copy(*step).wait_send()
    for step in mer_steps:
        out_copy(*step).wait()


def per_device(
    weather, windows, window_table, lon_gain, lon_qkv, lon_out, mer_gain, mer_qkv, mer_out,
    slopes, mlp_gain, mlp_in, mlp_out,
):
    vmem = pl.BlockSpec(memory_space=pltpu.VMEM)
    smem = pl.BlockSpec(memory_space=pltpu.SMEM)
    hbm = pl.BlockSpec(memory_space=pl.ANY)
    dma = pltpu.SemaphoreType.DMA
    return pl.pallas_call(
        kernel,
        out_shape=jax.ShapeDtypeStruct(weather.shape, BF16),
        in_specs=[hbm, smem, smem, vmem, vmem, vmem, smem] + [hbm] * 6,
        out_specs=hbm,
        scratch_shapes=[
            pltpu.VMEM((16, BLOCK, CH), BF16),
            pltpu.VMEM((4, BLOCK, 2048), BF16),
            pltpu.VMEM((8, 2048, BLOCK), BF16),
            pltpu.VMEM((4, 512, BLOCK), BF16),
            pltpu.VMEM((512, CH), BF16),
            pltpu.VMEM((2, 2, BLOCK, CH), BF16),
            pltpu.VMEM((16, 2, 16, CH), BF16),
            pltpu.VMEM((512, CH), F32),
            pltpu.VMEM((12, 512, BLOCK), BF16),
            pltpu.VMEM((16, 2, 16, CH), BF16),
            pltpu.VMEM((8, 2048), F32),
            pltpu.VMEM((256, 256), F32),
            pltpu.VMEM((512, 1536), BF16),
            pltpu.VMEM((512, 512), BF16),
            pltpu.VMEM((512, 1536), BF16),
            pltpu.VMEM((512, 512), BF16),
            pltpu.VMEM((512, 2048), BF16),
            pltpu.VMEM((2048, 512), BF16),
            dma((6,)), dma((3,)),
            dma((8,)), dma((8,)), dma((8,)), dma((8,)),
            dma((16,)), dma((16,)), dma((16,)), dma((16,)),
        ],
        compiler_params=pltpu.CompilerParams(
            collective_id=0, has_side_effects=True, vmem_limit_bytes=56 * 1024 * 1024
        ),
        name="axial",
    )(
        weather, windows, window_table,
        lon_gain.reshape(1, CH), mer_gain.reshape(1, CH), mlp_gain.reshape(1, CH), slopes,
        lon_qkv, lon_out, mer_qkv, mer_out, mlp_in, mlp_out,
    )


def solution(mesh):
    return jax.shard_map(
        per_device,
        mesh=mesh,
        in_specs=(
            P(None, "lat", "lon", None), P("lat"), P("lat", None),
            P(), P(), P(), P(), P(), P(), P(), P(), P(), P(),
        ),
        out_specs=P(None, "lat", "lon", None),
        check_vma=False,
    )
```

time: 848 us -> 75.4 us (0.09)
  waiting for transfers between devices: 446 us -> 0 us
  local copies, waits for them, and re-layouts: 160 us -> 1.87 us
  matrix products: 158 us -> 0 us
  Pallas kernels: 0 us -> 73.3 us
  other arithmetic: 52.4 us -> 0 us
  between operations: 13.4 us -> 0.01 us
  loops' own time: 11 us -> 0 us
    all_gather x4 -> x0, waiting for transfers between devices: 377 us -> none  [the longest x1 117 us: mer_gather(): partner_part = lax.all_gather(partner, 'lat', axis=1, tiled=True)]
    dot_general x58 -> x0, matrix products: 158 us -> none  [the longest x18 73.4 us: online_update(): jnp.einsum(pattern, weights.astype(jnp.bfloat16), values_part, preferred_...]
    pallas_call x0 -> x1, Pallas kernels: none -> 73.3 us  [per_device(): pl.pallas_call(kernel, out_shape=jax.ShapeDtypeStruct(weather.shape, BF16...]
    ppermute x1 -> x0, waiting for transfers between devices: 68.1 us -> none  [from_behind(): lax.ppermute(value, axis, [(i, (i + by) % devices) for i in range(devices)])]
    reshape x5 -> x0, local copies, waits for them, and re-layouts: 54.2 us -> none  [the longest x2 26.1 us: mer_gather(): member[..., :channels]]
    dynamic_slice x64 -> x0, local copies, waits for them, and re-layouts: 50.7 us -> none  [the longest x32 25.3 us: one_block(): lax.dynamic_slice_in_dim(values_all, first_cell, block_cells, 2)]
    reduce_sum x19 -> x0, other arithmetic: 50.2 us -> none  [the longest x18 48.8 us: online_update(): total_new = total_old * factor + jnp.sum(weights, axis=-1)]
    slice x12 -> x0, local copies, waits for them, and re-layouts: 40.4 us -> none  [the longest x4 24.3 us: mer_gather(): member[..., :channels]]
  transfers between devices with their start and end apart: 5 -> 0, of which waited for: 5 -> 0; matrix products, arithmetic and copies ran while one was open for 7% -> 0% of each run, Pallas kernels for 0% -> 0%
where the time goes in v1:
time: 75.4 us; the launch traced here: 75.2 us
  Pallas kernels  73.3 us (97%)
  local copies, waits for them, and re-layouts  1.87 us (2%)
    pallas_call x1, Pallas kernels, per_device(): pl.pallas_call(kernel, out_shape=jax.ShapeDtypeStruct(weather.shape, BF16...  73.3 us
    unnamed x1, local copies, waits for them, and re-layouts  1.87 us

profile of v1, /device:TPU:1, one launch (start us, length us, event | category | flops | bytes accessed | tf_op | source)
XLA Modules:
  0.0 75.2 jit_solution(15172409750525327186)
XLA Ops:
  0.0 73.3 %axial.1 = bf16[2,2,128,512]{3,2,1,0:T(8,128)(2,1)} custom-call(bf16[2,2,128,512]{3,2,1,0:T(8,128)(2,1)} %weather.1, s32[2]{0:T(128)} %windows.1, s32[2,16]{1,0:T(2,128)} %table.1, f32[1,512]{1,0:T(1,128)} %bitcast.3, f32[1,512]{1,0:T(1,128)} %bitcast.4, f32[1,512]{1,0:T(1,128)} %bitcast.5, f32[8]{0:T(128)} %slopes.1, bf16[512,1536]{1,0:T(8,128)(2,1)} %lon_qkv_h.1, ...), custom_call_target="tpu_custom_call" | custom-call | tf_op jit(solution)/shard_map/axial/pallas_call | solution.py:304
  73.3 1.9 %copy.15 = bf16[2,2,128,512]{3,2,1,0:T(8,128)(2,1)} copy(bf16[2,2,128,512]{3,2,1,0:T(8,128)(2,1)} %axial.1) | data formatting | bytes 1048576

commit v2 on v1

v2 whole, which is shorter than its diff:
```python
import functools

import jax
import jax.numpy as jnp
from jax import lax
from jax.experimental import pallas as pl
from jax.experimental.pallas import tpu as pltpu
from jax.sharding import PartitionSpec as P

MESH = pl.DeviceIdType.MESH
F32 = jnp.float32
BF16 = jnp.bfloat16
BLOCK = 128
CH = 512
NEG = -1e30
EPS = 1e-06


def rms(x, gain):
    inv = lax.rsqrt(jnp.mean(x * x, axis=-1, keepdims=True) + EPS)
    return (x * inv * gain).astype(BF16)


def dot(a, b):
    return jnp.dot(a, b, preferred_element_type=F32)


def dot_nt(a, b):
    return lax.dot_general(a, b, (((1,), (1,)), ((), ())), preferred_element_type=F32)


def kernel(
    weather, windows, table, lon_gain, mer_gain, mlp_gain, slopes,
    lon_qkv_h, lon_out_h, mer_qkv_h, mer_out_h, mlp_in_h, mlp_out_h,
    out,
    rowx, kt, vaug, qs, peak, accum, attn, mixed, merx, xg, mqkv, outs, bias, dist,
    lon_qkv, lon_out, mer_qkv, mer_out, mlp_in, mlp_out,
    w_sem, l_sem, lon_ss, lon_rs, fwd_ss, fwd_rs, mer_ss, mer_rs, out_ss, out_rs,
):
    lo, band = lax.axis_index("lon"), lax.axis_index("lat")
    zh, x, c = lo // 8, (lo // 2) % 4, lo % 2
    y, zl = band // 2, band % 2
    r = x % 2
    s = (x // 2 + zh) % 2

    def dev(zh, x, c, y, zl):
        return ((zh * 4 + x) * 2 + c, y * 2 + zl)

    def flip_x(e):
        return ((x // 2 + e // 2) % 2) * 2 + (x % 2 + e % 2) % 2

    loads = [
        pltpu.make_async_copy(src, dst, w_sem.at[i])
        for i, (src, dst) in enumerate(
            [(lon_qkv_h, lon_qkv), (lon_out_h, lon_out), (mer_qkv_h, mer_qkv),
             (mer_out_h, mer_out), (mlp_in_h, mlp_in), (mlp_out_h, mlp_out)]
        )
    ]
    own_copy = pltpu.make_async_copy(weather.at[s, r], rowx.at[0], l_sem.at[0])
    own_copy.start()
    loads[0].start()

    barrier = pltpu.get_barrier_semaphore()
    peers = [dev((zh + dz) % 2, flip_x(e), c, y, zl) for dz in range(2) for e in range(4) if dz + e]
    peers.append(dev(zh, x, 1 - c, y, zl))
    lat_steps = [(dy, dl) for dy in range(4) for dl in range(2)]
    peers += [
        dev(zh, flip_x(dr), c, (y + dy) % 4, (zl + dl) % 2)
        for dr in range(2) for dy, dl in lat_steps if dy + dl
    ]
    peers += [dev(1 - zh, x, c, (y + dy) % 4, (zl + dl) % 2) for dy, dl in lat_steps if dy + dl]
    for peer in peers:
        pl.semaphore_signal(barrier, inc=1, device_id=peer, device_id_type=MESH)
    pl.semaphore_wait(barrier, len(peers))

    def away(n):
        return (n // 2) % 2, n % 2 + 2 * (n // 4)

    def slot(n, handed):
        j = n // 2
        return (min(4 * j + 4, 14) if handed else max(4 * j - 2, 0)) + n % 2

    def lon_copy(n):
        dz, e = away(n)
        tz, tx = (zh + dz) % 2, flip_x(e)
        return pltpu.make_async_remote_copy(
            src_ref=weather.at[(tx // 2 + tz) % 2, tx % 2],
            dst_ref=rowx.at[slot(n, False)],
            send_sem=lon_ss.at[n],
            recv_sem=lon_rs.at[n],
            device_id=dev(tz, tx, c, y, zl),
            device_id_type=MESH,
        )

    def fwd_copy(n):
        return pltpu.make_async_remote_copy(
            src_ref=rowx.at[slot(n, False)],
            dst_ref=rowx.at[slot(n, True)],
            send_sem=fwd_ss.at[n],
            recv_sem=fwd_rs.at[n],
            device_id=dev(zh, x, 1 - c, y, zl),
            device_id_type=MESH,
        )

    for n in (2, 3, 1, 4, 5, 6, 7):
        lon_copy(n).start()
    own_copy.wait()
    fwd_copy(0).start()
    for load in loads[1:]:
        load.start()

    width = windows[r]
    rows_128 = lax.broadcasted_iota(jnp.int32, (BLOCK, BLOCK), 0)
    for n in range(8):
        for handed in range(2):
            dz, e = away(n)
            kb = ((zh + dz) % 2) * 8 + flip_x(e) * 2 + (c + handed) % 2
            value = jnp.zeros((BLOCK, BLOCK), F32)
            for qi in range(4):
                qb = ((zh + qi % 2) % 2) * 8 + flip_x(qi // 2) * 2 + c
                d = (kb - qb + 16) % 16
                seen = (jnp.minimum(d, 16 - d) <= width) & ((d == 0) | (table[r, d] == 1))
                value = jnp.where(rows_128 == qi, jnp.where(seen, 0.0, NEG), value)
            k0 = slot(n, handed) * BLOCK
            bias[:, k0 : k0 + BLOCK] = value.astype(BF16)

    def position(i):
        sl = i // 16
        row = (((y + sl // 4) % 4) * 2 + (zl + (sl // 2) % 2) % 2) * 2 + sl % 2
        half = ((i // 8) % 2 + zh) % 2
        return jnp.where(half == 0, row, 31 - row)

    ii = lax.broadcasted_iota(jnp.int32, (256, 256), 0)
    jj = lax.broadcasted_iota(jnp.int32, (256, 256), 1)
    apart = jnp.abs(position(ii) - position(jj))
    apart = jnp.minimum(apart, 32 - apart).astype(F32)
    dist[...] = jnp.where(ii % 8 == jj % 8, apart, -1.0)

    loads[0].wait()

    def keys_values(first, count):
        size = count * BLOCK
        normed = rms(rowx[first : first + count].reshape(size, CH).astype(F32), lon_gain[...])
        cells = slice(first * BLOCK, first * BLOCK + size)
        k = dot(normed, lon_qkv[:, CH : 2 * CH])
        kt[:, :, cells] = k.T.astype(BF16).reshape(4, BLOCK, size)
        v = dot(normed, lon_qkv[:, 2 * CH :]).astype(BF16)
        low = lax.broadcasted_iota(jnp.int32, (size, BLOCK), 1) < 64
        one = jnp.ones((size, BLOCK), BF16)
        for hp in range(4):
            part = v[:, hp * BLOCK : (hp + 1) * BLOCK]
            vaug[2 * hp, cells, :] = jnp.where(low, part, one)
            vaug[2 * hp + 1, cells, :] = jnp.where(low, one, part)
        return normed

    def queries(normed, dz):
        q = dot(normed, lon_qkv[:, :CH]).astype(BF16) * jnp.bfloat16(0.125)
        for e in range(2):
            for hp in range(4):
                r0 = (e * 2 + dz) * BLOCK
                qs[hp, r0 : r0 + BLOCK, :] = q[e * BLOCK : (e + 1) * BLOCK, hp * BLOCK : (hp + 1) * BLOCK]

    def attend(r0, size, first, count, begin=False, end=False):
        rows = slice(r0, r0 + size)
        cells = slice(first * BLOCK, (first + count) * BLOCK)
        low = lax.broadcasted_iota(jnp.int32, (size, BLOCK), 1) < 64
        none = jnp.zeros((size, BLOCK), BF16)
        block = lax.broadcasted_iota(jnp.int32, (size, BLOCK), 0) // BLOCK + r0 // BLOCK
        lane = lax.broadcasted_iota(jnp.int32, (size, BLOCK), 1)
        hot = jnp.where(block == lane, 1.0, 0.0).astype(BF16)

        @pl.loop(0, 4)
        def _(hp):
            qp = qs[hp, rows, :]
            kp = jnp.concatenate([kt[hp, :, cells], bias[:, cells]], axis=0)
            scores = [
                dot(jnp.concatenate([qm, hot], axis=1), kp)
                for qm in (jnp.where(low, qp, none), jnp.where(low, none, qp))
            ]
            res = []
            for hh in range(2):
                h = 2 * hp + hh
                m = jnp.max(scores[hh], axis=-1, keepdims=True)
                if not begin:
                    old = peak[h, rows, :][:, :1]
                    m = jnp.maximum(old, m)
                p = jnp.exp(scores[hh] - m).astype(BF16)
                o = dot(p, vaug[h, cells, :])
                if not begin:
                    o = accum[h, rows, :] * jnp.exp(old - m) + o
                if end:
                    res.append(o / pltpu.roll(o, 64, 1))
                else:
                    accum[h, rows, :] = o
                    peak[h, rows, :] = jnp.broadcast_to(m, (size, BLOCK))
            if end:
                attn[rows, pl.ds(pl.multiple_of(hp * BLOCK, BLOCK), BLOCK)] = jnp.where(
                    low, res[0], res[1]
                ).astype(BF16)

    lon_copy(1).wait_recv()
    fwd_copy(1).start()
    queries(keys_values(0, 2), 0)
    for n in (2, 3):
        lon_copy(n).wait_recv()
        fwd_copy(n).start()
    queries(keys_values(2, 2), 1)
    for n in (0, 1):
        fwd_copy(n).wait_recv()
    keys_values(4, 2)
    attend(0, 512, 0, 6, begin=True)
    for j in (2, 3):
        for n in (2 * j, 2 * j + 1):
            lon_copy(n).wait_recv()
            fwd_copy(n).start()
        for n in (2 * j - 2, 2 * j - 1):
            fwd_copy(n).wait_recv()
        keys_values(4 * j - 2, 4)
        attend(0, 512, 4 * j - 2, 4)
    for n in (6, 7):
        fwd_copy(n).wait_recv()
    keys_values(14, 2)
    loads[1].wait()

    def mer_copy(dr, dy, dl):
        ty, tl = (y + dy) % 4, (zl + dl) % 2
        n = (dr * 4 + dy) * 2 + dl
        src = mixed.at[dr, :, pl.ds(pl.multiple_of((ty * 2 + tl) * 16, 16), 16), :]
        dst = merx.at[(((4 - dy) % 4) * 2 + dl) * 2 + r]
        if n == 0:
            return pltpu.make_async_copy(src, dst, l_sem.at[1])
        return pltpu.make_async_remote_copy(
            src_ref=src, dst_ref=dst, send_sem=mer_ss.at[n], recv_sem=mer_rs.at[n],
            device_id=dev(zh, flip_x(dr), c, ty, tl), device_id_type=MESH,
        )

    mer_steps = [(dr, dy, dl) for dr in range(2) for dy, dl in lat_steps]
    for e in (1, 0):
        attend(e * 256, 256, 14, 2, end=True)
        new = dot(attn[e * 256 : (e + 1) * 256, :], lon_out[...])
        for dz in range(2):
            part = rowx[2 * dz + e].astype(F32) + new[dz * BLOCK : (dz + 1) * BLOCK]
            mixed[e, dz] = part.astype(BF16)
        for dy, dl in lat_steps[::-1]:
            mer_copy(e, dy, dl).start()
    for load in loads[2:]:
        load.wait()
    for step in mer_steps:
        if sum(step):
            mer_copy(*step).wait_recv()
        else:
            mer_copy(*step).wait()

    low_256 = lax.broadcasted_iota(jnp.int32, (256, BLOCK), 1) < 64
    none = jnp.zeros((256, BLOCK), BF16)
    cells = merx[...].astype(F32).reshape(32, 2, 8, CH)
    for g in range(2):
        part = cells[:, g].reshape(256, CH)
        xg[g * 256 : (g + 1) * 256, :] = part
        qkv = dot(rms(part, mer_gain[...]), mer_qkv[...]).astype(BF16)
        for j in range(12):
            mqkv[j, g * 256 : (g + 1) * 256, :] = qkv[:, j * BLOCK : (j + 1) * BLOCK]

    ones_256 = jnp.ones((256, BLOCK), BF16)

    @pl.loop(0, 4)
    def _(hp):
        far = dist[...]
        units = [(g, hh) for g in range(2) for hh in range(2)]
        scores = []
        for g, hh in units:
            rows = slice(g * 256, (g + 1) * 256)
            qp = mqkv[hp, rows, :] * jnp.bfloat16(0.125)
            qm = jnp.where(low_256, qp, none) if hh == 0 else jnp.where(low_256, none, qp)
            scores.append(dot_nt(qm, mqkv[4 + hp, rows, :]))
        res = []
        for (g, hh), sc in zip(units, scores):
            vp = mqkv[8 + hp, g * 256 : (g + 1) * 256, :]
            vm = jnp.where(low_256, vp, ones_256) if hh == 0 else jnp.where(low_256, ones_256, vp)
            sc = jnp.where(far >= 0.0, sc - far * slopes[2 * hp + hh], NEG)
            m = jnp.max(sc, axis=-1, keepdims=True)
            p = jnp.exp(sc - m).astype(BF16)
            o = dot(p, vm)
            res.append(o / pltpu.roll(o, 64, 1))
        for g in range(2):
            attn[g * 256 : (g + 1) * 256, pl.ds(pl.multiple_of(hp * BLOCK, BLOCK), BLOCK)] = jnp.where(
                low_256, res[2 * g], res[2 * g + 1]
            ).astype(BF16)

    for g in range(2):
        rows = slice(g * 256, (g + 1) * 256)
        mm = (xg[rows, :] + dot(attn[rows, :], mer_out[...])).astype(BF16).astype(F32)
        normed = rms(mm, mlp_gain[...])
        xg[rows, :] = mm
        attn[rows, :] = normed

    @pl.loop(0, 4)
    def _(j):
        cols = pl.ds(pl.multiple_of(j * CH, CH), CH)
        hidden = jax.nn.gelu(dot(attn[...], mlp_in[:, cols])).astype(BF16)
        xg[...] += dot(hidden, mlp_out[cols, :])

    done = jnp.swapaxes(xg[...].reshape(2, 32, 8, CH), 0, 1)
    outs[...] = done.reshape(16, 2, 16, CH).astype(BF16)

    def out_copy(dz, dy, dl):
        tz, ty, tl = (zh + dz) % 2, (y + dy) % 4, (zl + dl) % 2
        n = (dz * 4 + dy) * 2 + dl
        src = outs.at[pl.ds((dy * 2 + dl) * 2, 2), dz]
        dst = out.at[s, :, pl.ds(pl.multiple_of(band * 16, 16), 16), :]
        if n == 0:
            return pltpu.make_async_copy(src, dst, l_sem.at[2])
        return pltpu.make_async_remote_copy(
            src_ref=src, dst_ref=dst, send_sem=out_ss.at[n], recv_sem=out_rs.at[n],
            device_id=dev(tz, x, c, ty, tl), device_id_type=MESH,
        )

    for step in mer_steps:
        out_copy(*step).start()
    for n in range(1, 8):
        lon_copy(n).wait_send()
    for n in range(8):
        fwd_copy(n).wait_send()
    for step in mer_steps:
        if sum(step):
            mer_copy(*step).wait_send()
    for step in mer_steps:
        out_copy(*step).wait()


def per_device(
    weather, windows, window_table, lon_gain, lon_qkv, lon_out, mer_gain, mer_qkv, mer_out,
    slopes, mlp_gain, mlp_in, mlp_out,
):
    vmem = pl.BlockSpec(memory_space=pltpu.VMEM)
    smem = pl.BlockSpec(memory_space=pltpu.SMEM)
    hbm = pl.BlockSpec(memory_space=pl.ANY)
    dma = pltpu.SemaphoreType.DMA
    return pl.pallas_call(
        kernel,
        out_shape=jax.ShapeDtypeStruct(weather.shape, BF16),
        in_specs=[hbm, smem, smem, vmem, vmem, vmem, smem] + [hbm] * 6,
        out_specs=hbm,
        scratch_shapes=[
            pltpu.VMEM((16, BLOCK, CH), BF16),
            pltpu.VMEM((4, BLOCK, 2048), BF16),
            pltpu.VMEM((8, 2048, BLOCK), BF16),
            pltpu.VMEM((4, 512, BLOCK), BF16),
            pltpu.VMEM((8, 512, BLOCK), F32),
            pltpu.VMEM((8, 512, BLOCK), F32),
            pltpu.VMEM((512, CH), BF16),
            pltpu.VMEM((2, 2, BLOCK, CH), BF16),
            pltpu.VMEM((16, 2, 16, CH), BF16),
            pltpu.VMEM((512, CH), F32),
            pltpu.VMEM((12, 512, BLOCK), BF16),
            pltpu.VMEM((16, 2, 16, CH), BF16),
            pltpu.VMEM((BLOCK, 2048), BF16),
            pltpu.VMEM((256, 256), F32),
            pltpu.VMEM((512, 1536), BF16),
            pltpu.VMEM((512, 512), BF16),
            pltpu.VMEM((512, 1536), BF16),
            pltpu.VMEM((512, 512), BF16),
            pltpu.VMEM((512, 2048), BF16),
            pltpu.VMEM((2048, 512), BF16),
            dma((6,)), dma((3,)),
            dma((8,)), dma((8,)), dma((8,)), dma((8,)),
            dma((16,)), dma((16,)), dma((16,)), dma((16,)),
        ],
        compiler_params=pltpu.CompilerParams(
            collective_id=0, has_side_effects=True, vmem_limit_bytes=56 * 1024 * 1024
        ),
        name="axial",
    )(
        weather, windows, window_table,
        lon_gain.reshape(1, CH), mer_gain.reshape(1, CH), mlp_gain.reshape(1, CH), slopes,
        lon_qkv, lon_out, mer_qkv, mer_out, mlp_in, mlp_out,
    )


def solution(mesh):
    return jax.shard_map(
        per_device,
        mesh=mesh,
        in_specs=(
            P(None, "lat", "lon", None), P("lat"), P("lat", None),
            P(), P(), P(), P(), P(), P(), P(), P(), P(), P(),
        ),
        out_specs=P(None, "lat", "lon", None),
        check_vma=False,
    )
```

time: 75.4 us -> 77.6 us (1.029)
  Pallas kernels: 73.3 us -> 75.5 us
    pallas_call x1, Pallas kernels: 73.3 us -> 75.5 us  [per_device(): pl.pallas_call(kernel, out_shape=jax.ShapeDtypeStruct(weather.shape, BF16...]
where the time goes in v2:
time: 77.6 us; the launch traced here: 77.4 us
  Pallas kernels  75.5 us (97%)
  local copies, waits for them, and re-layouts  1.87 us (2%)
    pallas_call x1, Pallas kernels, per_device(): pl.pallas_call(kernel, out_shape=jax.ShapeDtypeStruct(weather.shape, BF16...  75.5 us
    unnamed x1, local copies, waits for them, and re-layouts  1.87 us

profile of v2, /device:TPU:1, one launch (start us, length us, event | category | flops | bytes accessed | tf_op | source)
XLA Modules:
  0.0 77.4 jit_solution(15456215003996382875)
XLA Ops:
  0.0 75.5 %axial.1 = bf16[2,2,128,512]{3,2,1,0:T(8,128)(2,1)} custom-call(bf16[2,2,128,512]{3,2,1,0:T(8,128)(2,1)} %weather.1, s32[2]{0:T(128)} %windows.1, s32[2,16]{1,0:T(2,128)} %table.1, f32[1,512]{1,0:T(1,128)} %bitcast.3, f32[1,512]{1,0:T(1,128)} %bitcast.4, f32[1,512]{1,0:T(1,128)} %bitcast.5, f32[8]{0:T(128)} %slopes.1, bf16[512,1536]{1,0:T(8,128)(2,1)} %lon_qkv_h.1, ...), custom_call_target="tpu_custom_call" | custom-call | tf_op jit(solution)/shard_map/axial/pallas_call | solution.py:339
  75.5 1.9 %copy.15 = bf16[2,2,128,512]{3,2,1,0:T(8,128)(2,1)} copy(bf16[2,2,128,512]{3,2,1,0:T(8,128)(2,1)} %axial.1) | data formatting | bytes 1048576

commit v3 on v2

--- a/solution.py
+++ b/solution.py
@@ -102,7 +102,7 @@
             device_id_type=MESH,
         )
 
-    for n in (2, 3, 1, 4, 5, 6, 7):
+    for n in (2, 1, 3, 5):
         lon_copy(n).start()
     own_copy.wait()
     fwd_copy(0).start()
@@ -160,7 +160,7 @@
                 r0 = (e * 2 + dz) * BLOCK
                 qs[hp, r0 : r0 + BLOCK, :] = q[e * BLOCK : (e + 1) * BLOCK, hp * BLOCK : (hp + 1) * BLOCK]
 
-    def attend(r0, size, first, count, begin=False, end=False):
+    def attend(r0, size, first, count, heads, begin=False, end=False):
         rows = slice(r0, r0 + size)
         cells = slice(first * BLOCK, (first + count) * BLOCK)
         low = lax.broadcasted_iota(jnp.int32, (size, BLOCK), 1) < 64
@@ -169,54 +169,73 @@
         lane = lax.broadcasted_iota(jnp.int32, (size, BLOCK), 1)
         hot = jnp.where(block == lane, 1.0, 0.0).astype(BF16)
 
-        @pl.loop(0, 4)
-        def _(hp):
+        def score(hp, hh):
             qp = qs[hp, rows, :]
+            qm = jnp.where(low, none, qp) if hh else jnp.where(low, qp, none)
             kp = jnp.concatenate([kt[hp, :, cells], bias[:, cells]], axis=0)
-            scores = [
-                dot(jnp.concatenate([qm, hot], axis=1), kp)
-                for qm in (jnp.where(low, qp, none), jnp.where(low, none, qp))
-            ]
+            return dot(jnp.concatenate([qm, hot], axis=1), kp)
+
+        @pl.loop(heads[0], heads[1], step=2)
+        def _(pair):
+            units = [(pair + j, hh) for j in range(2) for hh in range(2)]
+            ahead = score(*units[0])
             res = []
-            for hh in range(2):
+            for i, (hp, hh) in enumerate(units):
+                sc = ahead
+                if i + 1 < len(units):
+                    ahead = score(*units[i + 1])
                 h = 2 * hp + hh
-                m = jnp.max(scores[hh], axis=-1, keepdims=True)
-                if not begin:
-                    old = peak[h, rows, :][:, :1]
+                m = jnp.max(sc, axis=-1, keepdims=True)
+                if begin:
+                    p = jnp.exp(sc - m).astype(BF16)
+                    o = dot(p, vaug[h, cells, :])
+                else:
+                    old = peak[h, rows, :]
                     m = jnp.maximum(old, m)
-                p = jnp.exp(scores[hh] - m).astype(BF16)
-                o = dot(p, vaug[h, cells, :])
-                if not begin:
+                    p = [jnp.exp(sc[:, j * BLOCK : (j + 1) * BLOCK] - m).astype(BF16) for j in range(count)]
+                    o = dot(jnp.concatenate(p, axis=1), vaug[h, cells, :])
                     o = accum[h, rows, :] * jnp.exp(old - m) + o
                 if end:
                     res.append(o / pltpu.roll(o, 64, 1))
+                    if hh:
+                        attn[rows, pl.ds(pl.multiple_of(hp * BLOCK, BLOCK), BLOCK)] = jnp.where(
+                            low, res[-2], res[-1]
+                        ).astype(BF16)
                 else:
                     accum[h, rows, :] = o
                     peak[h, rows, :] = jnp.broadcast_to(m, (size, BLOCK))
-            if end:
-                attn[rows, pl.ds(pl.multiple_of(hp * BLOCK, BLOCK), BLOCK)] = jnp.where(
-                    low, res[0], res[1]
-                ).astype(BF16)
 
     lon_copy(1).wait_recv()
     fwd_copy(1).start()
     queries(keys_values(0, 2), 0)
-    for n in (2, 3):
-        lon_copy(n).wait_recv()
-        fwd_copy(n).start()
-    queries(keys_values(2, 2), 1)
+    for n in (1, 2):
+        lon_copy(n).wait_send()
+    for n in (4, 7, 6):
+        lon_copy(n).start()
+    lon_copy(2).wait_recv()
+    fwd_copy(2).start()
     for n in (0, 1):
         fwd_copy(n).wait_recv()
     keys_values(4, 2)
-    attend(0, 512, 0, 6, begin=True)
-    for j in (2, 3):
-        for n in (2 * j, 2 * j + 1):
-            lon_copy(n).wait_recv()
-            fwd_copy(n).start()
-        for n in (2 * j - 2, 2 * j - 1):
-            fwd_copy(n).wait_recv()
-        keys_values(4 * j - 2, 4)
-        attend(0, 512, 4 * j - 2, 4)
+    lon_copy(3).wait_recv()
+    fwd_copy(3).start()
+    queries(keys_values(2, 2), 1)
+    attend(0, 512, 0, 6, (0, 2), begin=True)
+    lon_copy(5).wait_recv()
+    fwd_copy(5).start()
+    attend(0, 512, 0, 6, (2, 4), begin=True)
+    lon_copy(4).wait_recv()
+    fwd_copy(4).start()
+    for n in (2, 3):
+        fwd_copy(n).wait_recv()
+    keys_values(6, 4)
+    attend(0, 512, 6, 4, (0, 4))
+    for n in (6, 7):
+        lon_copy(n).wait_recv()
+        fwd_copy(n).start()
+    for n in (4, 5):
+        fwd_copy(n).wait_recv()
+    keys_values(10, 4)
     for n in (6, 7):
         fwd_copy(n).wait_recv()
     keys_values(14, 2)
@@ -236,7 +255,7 @@
 
     mer_steps = [(dr, dy, dl) for dr in range(2) for dy, dl in lat_steps]
     for e in (1, 0):
-        attend(e * 256, 256, 14, 2, end=True)
+        attend(e * 256, 256, 10, 6, (0, 4), end=True)
         new = dot(attn[e * 256 : (e + 1) * 256, :], lon_out[...])
         for dz in range(2):
             part = rowx[2 * dz + e].astype(F32) + new[dz * BLOCK : (dz + 1) * BLOCK]
@@ -317,7 +336,7 @@
 
     for step in mer_steps:
         out_copy(*step).start()
-    for n in range(1, 8):
+    for n in (3, 4, 5, 6, 7):
         lon_copy(n).wait_send()
     for n in range(8):
         fwd_copy(n).wait_send()

time: 77.6 us -> 63.8 us (0.82)
  Pallas kernels: 75.5 us -> 61.5 us
    pallas_call x1, Pallas kernels: 75.5 us -> 61.5 us  [per_device(): pl.pallas_call(kernel, out_shape=jax.ShapeDtypeStruct(weather.shape, BF16...]
where the time goes in v3:
time: 63.8 us; the launch traced here: 63.3 us
  Pallas kernels  61.5 us (96%)
  local copies, waits for them, and re-layouts  1.87 us (3%)
    pallas_call x1, Pallas kernels, per_device(): pl.pallas_call(kernel, out_shape=jax.ShapeDtypeStruct(weather.shape, BF16...  61.5 us
    unnamed x1, local copies, waits for them, and re-layouts  1.87 us

profile of v3, /device:TPU:1, one launch (start us, length us, event | category | flops | bytes accessed | tf_op | source)
XLA Modules:
  0.0 63.3 jit_solution(15481789252346742273)
XLA Ops:
  0.0 61.5 %axial.1 = bf16[2,2,128,512]{3,2,1,0:T(8,128)(2,1)} custom-call(bf16[2,2,128,512]{3,2,1,0:T(8,128)(2,1)} %weather.1, s32[2]{0:T(128)} %windows.1, s32[2,16]{1,0:T(2,128)} %table.1, f32[1,512]{1,0:T(1,128)} %bitcast.3, f32[1,512]{1,0:T(1,128)} %bitcast.4, f32[1,512]{1,0:T(1,128)} %bitcast.5, f32[8]{0:T(128)} %slopes.1, bf16[512,1536]{1,0:T(8,128)(2,1)} %lon_qkv_h.1, ...), custom_call_target="tpu_custom_call" | custom-call | tf_op jit(solution)/shard_map/axial/pallas_call | solution.py:358
  61.5 1.9 %copy.15 = bf16[2,2,128,512]{3,2,1,0:T(8,128)(2,1)} copy(bf16[2,2,128,512]{3,2,1,0:T(8,128)(2,1)} %axial.1) | data formatting | bytes 1048576

commit v4 on v3

--- a/solution.py
+++ b/solution.py
@@ -124,9 +124,13 @@
             k0 = slot(n, handed) * BLOCK
             bias[:, k0 : k0 + BLOCK] = value.astype(BF16)
 
+    def piece_at(dr, dy, dl):
+        near = 0 if dy in (1, 2) else 1
+        return near * 8 + dr * 4 + ((dy - 1 - 2 * near) % 4) * 2 + dl
+
     def position(i):
-        sl = i // 16
-        row = (((y + sl // 4) % 4) * 2 + (zl + (sl // 2) % 2) % 2) * 2 + sl % 2
+        near, dr, dyi, dl = i // 128, (i // 64) % 2, (i // 32) % 2, (i // 16) % 2
+        row = (((y + 1 + 2 * near + dyi) % 4) * 2 + (zl + dl) % 2) * 2 + (r + dr) % 2
         half = ((i // 8) % 2 + zh) % 2
         return jnp.where(half == 0, row, 31 - row)
 
@@ -223,16 +227,17 @@
     attend(0, 512, 0, 6, (0, 2), begin=True)
     lon_copy(5).wait_recv()
     fwd_copy(5).start()
-    attend(0, 512, 0, 6, (2, 4), begin=True)
     lon_copy(4).wait_recv()
     fwd_copy(4).start()
+    attend(0, 512, 0, 6, (2, 4), begin=True)
     for n in (2, 3):
         fwd_copy(n).wait_recv()
     keys_values(6, 4)
-    attend(0, 512, 6, 4, (0, 4))
+    attend(0, 512, 6, 4, (0, 2))
     for n in (6, 7):
         lon_copy(n).wait_recv()
         fwd_copy(n).start()
+    attend(0, 512, 6, 4, (2, 4))
     for n in (4, 5):
         fwd_copy(n).wait_recv()
     keys_values(10, 4)
@@ -245,7 +250,7 @@
         ty, tl = (y + dy) % 4, (zl + dl) % 2
         n = (dr * 4 + dy) * 2 + dl
         src = mixed.at[dr, :, pl.ds(pl.multiple_of((ty * 2 + tl) * 16, 16), 16), :]
-        dst = merx.at[(((4 - dy) % 4) * 2 + dl) * 2 + r]
+        dst = merx.at[piece_at(dr, (4 - dy) % 4, dl)]
         if n == 0:
             return pltpu.make_async_copy(src, dst, l_sem.at[1])
         return pltpu.make_async_remote_copy(
@@ -264,68 +269,64 @@
             mer_copy(e, dy, dl).start()
     for load in loads[2:]:
         load.wait()
-    for step in mer_steps:
-        if sum(step):
-            mer_copy(*step).wait_recv()
-        else:
-            mer_copy(*step).wait()
+    for dr in (1, 0):
+        for dy, dl in lat_steps:
+            if dr + dy + dl:
+                mer_copy(dr, dy, dl).wait_recv()
+            else:
+                mer_copy(dr, dy, dl).wait()
+        parts = [[], []]
+        for near in range(2):
+            p0 = near * 8 + dr * 4
+            cells = merx[p0 : p0 + 4].astype(F32).reshape(8, 2, 8, CH)
+            for g in range(2):
+                parts[g].append(cells[:, g].reshape(64, CH))
+        cells = jnp.concatenate(parts[0] + parts[1], axis=0)
+        qkv = dot(rms(cells, mer_gain[...]), mer_qkv[...]).astype(BF16)
+        for q in range(4):
+            r0 = (q // 2) * 256 + (q % 2) * 128 + dr * 64
+            xg[r0 : r0 + 64, :] = cells[q * 64 : (q + 1) * 64]
+            for j in range(12):
+                mqkv[j, r0 : r0 + 64, :] = qkv[q * 64 : (q + 1) * 64, j * BLOCK : (j + 1) * BLOCK]
 
     low_256 = lax.broadcasted_iota(jnp.int32, (256, BLOCK), 1) < 64
     none = jnp.zeros((256, BLOCK), BF16)
-    cells = merx[...].astype(F32).reshape(32, 2, 8, CH)
-    for g in range(2):
-        part = cells[:, g].reshape(256, CH)
-        xg[g * 256 : (g + 1) * 256, :] = part
-        qkv = dot(rms(part, mer_gain[...]), mer_qkv[...]).astype(BF16)
-        for j in range(12):
-            mqkv[j, g * 256 : (g + 1) * 256, :] = qkv[:, j * BLOCK : (j + 1) * BLOCK]
-
     ones_256 = jnp.ones((256, BLOCK), BF16)
 
     @pl.loop(0, 4)
     def _(hp):
         far = dist[...]
-        units = [(g, hh) for g in range(2) for hh in range(2)]
-        scores = []
-        for g, hh in units:
+        units = [(hp, g, hh) for g in range(2) for hh in range(2)]
+
+        def score(hp, g, hh):
             rows = slice(g * 256, (g + 1) * 256)
             qp = mqkv[hp, rows, :] * jnp.bfloat16(0.125)
-            qm = jnp.where(low_256, qp, none) if hh == 0 else jnp.where(low_256, none, qp)
-            scores.append(dot_nt(qm, mqkv[4 + hp, rows, :]))
+            return dot_nt(jnp.where(low_256, none, qp) if hh else jnp.where(low_256, qp, none), mqkv[4 + hp, rows, :])
+
+        ahead = [score(*units[0]), score(*units[1])]
         res = []
-        for (g, hh), sc in zip(units, scores):
-            vp = mqkv[8 + hp, g * 256 : (g + 1) * 256, :]
-            vm = jnp.where(low_256, vp, ones_256) if hh == 0 else jnp.where(low_256, ones_256, vp)
+        for i, (hp, g, hh) in enumerate(units):
+            sc = ahead.pop(0)
+            if i + 2 < len(units):
+                ahead.append(score(*units[i + 2]))
+            rows = slice(g * 256, (g + 1) * 256)
+            vp = mqkv[8 + hp, rows, :]
+            vm = jnp.where(low_256, ones_256, vp) if hh else jnp.where(low_256, vp, ones_256)
             sc = jnp.where(far >= 0.0, sc - far * slopes[2 * hp + hh], NEG)
             m = jnp.max(sc, axis=-1, keepdims=True)
             p = jnp.exp(sc - m).astype(BF16)
             o = dot(p, vm)
             res.append(o / pltpu.roll(o, 64, 1))
-        for g in range(2):
-            attn[g * 256 : (g + 1) * 256, pl.ds(pl.multiple_of(hp * BLOCK, BLOCK), BLOCK)] = jnp.where(
-                low_256, res[2 * g], res[2 * g + 1]
-            ).astype(BF16)
-
-    for g in range(2):
-        rows = slice(g * 256, (g + 1) * 256)
-        mm = (xg[rows, :] + dot(attn[rows, :], mer_out[...])).astype(BF16).astype(F32)
-        normed = rms(mm, mlp_gain[...])
-        xg[rows, :] = mm
-        attn[rows, :] = normed
-
-    @pl.loop(0, 4)
-    def _(j):
-        cols = pl.ds(pl.multiple_of(j * CH, CH), CH)
-        hidden = jax.nn.gelu(dot(attn[...], mlp_in[:, cols])).astype(BF16)
-        xg[...] += dot(hidden, mlp_out[cols, :])
-
-    done = jnp.swapaxes(xg[...].reshape(2, 32, 8, CH), 0, 1)
-    outs[...] = done.reshape(16, 2, 16, CH).astype(BF16)
+            if hh:
+                attn[rows, pl.ds(pl.multiple_of(hp * BLOCK, BLOCK), BLOCK)] = jnp.where(
+                    low_256, res[-2], res[-1]
+                ).astype(BF16)
 
     def out_copy(dz, dy, dl):
         tz, ty, tl = (zh + dz) % 2, (y + dy) % 4, (zl + dl) % 2
         n = (dz * 4 + dy) * 2 + dl
-        src = outs.at[pl.ds((dy * 2 + dl) * 2, 2), dz]
+        piece = piece_at(0, dy, dl)
+        src = outs.at[piece // 8, :, piece % 4, dz]
         dst = out.at[s, :, pl.ds(pl.multiple_of(band * 16, 16), 16), :]
         if n == 0:
             return pltpu.make_async_copy(src, dst, l_sem.at[2])
@@ -334,8 +335,32 @@
             device_id=dev(tz, x, c, ty, tl), device_id_type=MESH,
         )
 
-    for step in mer_steps:
-        out_copy(*step).start()
+    for near in range(2):
+        halves = []
+        for g in range(2):
+            r0 = g * 256 + near * 128
+            halves.append(xg[r0 : r0 + 128, :] + dot(attn[r0 : r0 + 128, :], mer_out[...]))
+        mm = jnp.concatenate([h.reshape(16, 1, 8, CH) for h in halves], axis=1).reshape(256, CH)
+        mm = mm.astype(BF16).astype(F32)
+        normed = rms(mm, mlp_gain[...])
+
+        def up(j):
+            return dot(normed, mlp_in[:, j * CH : (j + 1) * CH])
+
+        ahead = up(0)
+        for j in range(4):
+            hidden = ahead
+            if j < 3:
+                ahead = up(j + 1)
+            mm = mm + dot(jax.nn.gelu(hidden).astype(BF16), mlp_out[j * CH : (j + 1) * CH, :])
+        mm = mm.astype(BF16).reshape(2, 4, 2, 16, CH)
+        for dr in range(2):
+            outs[near, (r + dr) % 2] = mm[dr]
+        for dy in ((2, 1), (3, 0))[near]:
+            for dz in (1, 0):
+                for dl in (1, 0):
+                    out_copy(dz, dy, dl).start()
+
     for n in (3, 4, 5, 6, 7):
         lon_copy(n).wait_send()
     for n in range(8):
@@ -372,7 +397,7 @@
             pltpu.VMEM((16, 2, 16, CH), BF16),
             pltpu.VMEM((512, CH), F32),
             pltpu.VMEM((12, 512, BLOCK), BF16),
-            pltpu.VMEM((16, 2, 16, CH), BF16),
+            pltpu.VMEM((2, 2, 4, 2, 16, CH), BF16),
             pltpu.VMEM((BLOCK, 2048), BF16),
             pltpu.VMEM((256, 256), F32),
             pltpu.VMEM((512, 1536), BF16),

time: 63.8 us -> 58.4 us (0.915)
  Pallas kernels: 61.5 us -> 56.3 us
    pallas_call x1, Pallas kernels: 61.5 us -> 56.3 us  [per_device(): pl.pallas_call(kernel, out_shape=jax.ShapeDtypeStruct(weather.shape, BF16...]
where the time goes in v4:
time: 58.4 us; the launch traced here: 58.2 us
  Pallas kernels  56.3 us (96%)
  local copies, waits for them, and re-layouts  1.87 us (3%)
    pallas_call x1, Pallas kernels, per_device(): pl.pallas_call(kernel, out_shape=jax.ShapeDtypeStruct(weather.shape, BF16...  56.3 us
    unnamed x1, local copies, waits for them, and re-layouts  1.87 us

profile of v4, /device:TPU:1, one launch (start us, length us, event | category | flops | bytes accessed | tf_op | source)
XLA Modules:
  0.0 58.2 jit_solution(9204223987456740638)
XLA Ops:
  0.0 56.3 %axial.1 = bf16[2,2,128,512]{3,2,1,0:T(8,128)(2,1)} custom-call(bf16[2,2,128,512]{3,2,1,0:T(8,128)(2,1)} %weather.1, s32[2]{0:T(128)} %windows.1, s32[2,16]{1,0:T(2,128)} %table.1, f32[1,512]{1,0:T(1,128)} %bitcast.3, f32[1,512]{1,0:T(1,128)} %bitcast.4, f32[1,512]{1,0:T(1,128)} %bitcast.5, f32[8]{0:T(128)} %slopes.1, bf16[512,1536]{1,0:T(8,128)(2,1)} %lon_qkv_h.1, ...), custom_call_target="tpu_custom_call" | custom-call | tf_op jit(solution)/shard_map/axial/pallas_call | solution.py:383
  56.3 1.9 %copy.15 = bf16[2,2,128,512]{3,2,1,0:T(8,128)(2,1)} copy(bf16[2,2,128,512]{3,2,1,0:T(8,128)(2,1)} %axial.1) | data formatting | bytes 1048576

commit v5 on v4

--- a/solution.py
+++ b/solution.py
@@ -77,8 +77,7 @@
         return (n // 2) % 2, n % 2 + 2 * (n // 4)
 
     def slot(n, handed):
-        j = n // 2
-        return (min(4 * j + 4, 14) if handed else max(4 * j - 2, 0)) + n % 2
+        return ((4, 8, 10, 14) if handed else (0, 2, 6, 12))[n // 2] + n % 2
 
     def lon_copy(n):
         dz, e = away(n)
@@ -175,9 +174,16 @@
 
         def score(hp, hh):
             qp = qs[hp, rows, :]
-            qm = jnp.where(low, none, qp) if hh else jnp.where(low, qp, none)
+            qms = [jnp.where(low, qp, none), jnp.where(low, none, qp)]
             kp = jnp.concatenate([kt[hp, :, cells], bias[:, cells]], axis=0)
-            return dot(jnp.concatenate([qm, hot], axis=1), kp)
+            if not end:
+                return dot(jnp.concatenate([qms[hh], hot], axis=1), kp)
+            if hh == 0:
+                both = jnp.concatenate([jnp.concatenate([qm, hot], axis=1) for qm in qms], axis=0)
+                stacked.append(dot(both, kp))
+            return stacked[-1][hh * size : (hh + 1) * size]
+
+        stacked = []
 
         @pl.loop(heads[0], heads[1], step=2)
         def _(pair):
@@ -233,14 +239,15 @@
     for n in (2, 3):
         fwd_copy(n).wait_recv()
     keys_values(6, 4)
-    attend(0, 512, 6, 4, (0, 2))
+    for n in (4, 5):
+        fwd_copy(n).wait_recv()
+    keys_values(10, 2)
+    attend(0, 512, 6, 6, (0, 2))
     for n in (6, 7):
         lon_copy(n).wait_recv()
         fwd_copy(n).start()
-    attend(0, 512, 6, 4, (2, 4))
-    for n in (4, 5):
-        fwd_copy(n).wait_recv()
-    keys_values(10, 4)
+    attend(0, 512, 6, 6, (2, 4))
+    keys_values(12, 2)
     for n in (6, 7):
         fwd_copy(n).wait_recv()
     keys_values(14, 2)
@@ -260,7 +267,7 @@
 
     mer_steps = [(dr, dy, dl) for dr in range(2) for dy, dl in lat_steps]
     for e in (1, 0):
-        attend(e * 256, 256, 10, 6, (0, 4), end=True)
+        attend(e * 256, 256, 12, 4, (0, 4), end=True)
         new = dot(attn[e * 256 : (e + 1) * 256, :], lon_out[...])
         for dz in range(2):
             part = rowx[2 * dz + e].astype(F32) + new[dz * BLOCK : (dz + 1) * BLOCK]
@@ -296,31 +303,25 @@
     @pl.loop(0, 4)
     def _(hp):
         far = dist[...]
-        units = [(hp, g, hh) for g in range(2) for hh in range(2)]
-
-        def score(hp, g, hh):
+        scores = []
+        for g in range(2):
             rows = slice(g * 256, (g + 1) * 256)
             qp = mqkv[hp, rows, :] * jnp.bfloat16(0.125)
-            return dot_nt(jnp.where(low_256, none, qp) if hh else jnp.where(low_256, qp, none), mqkv[4 + hp, rows, :])
-
-        ahead = [score(*units[0]), score(*units[1])]
-        res = []
-        for i, (hp, g, hh) in enumerate(units):
-            sc = ahead.pop(0)
-            if i + 2 < len(units):
-                ahead.append(score(*units[i + 2]))
+            both = jnp.concatenate([jnp.where(low_256, qp, none), jnp.where(low_256, none, qp)], axis=0)
+            scores.append(dot_nt(both, mqkv[4 + hp, rows, :]))
+        for g in range(2):
             rows = slice(g * 256, (g + 1) * 256)
-            vp = mqkv[8 + hp, rows, :]
-            vm = jnp.where(low_256, ones_256, vp) if hh else jnp.where(low_256, vp, ones_256)
-            sc = jnp.where(far >= 0.0, sc - far * slopes[2 * hp + hh], NEG)
-            m = jnp.max(sc, axis=-1, keepdims=True)
-            p = jnp.exp(sc - m).astype(BF16)
-            o = dot(p, vm)
-            res.append(o / pltpu.roll(o, 64, 1))
-            if hh:
-                attn[rows, pl.ds(pl.multiple_of(hp * BLOCK, BLOCK), BLOCK)] = jnp.where(
-                    low_256, res[-2], res[-1]
-                ).astype(BF16)
+            p = []
+            for hh in range(2):
+                sc = scores[g][hh * 256 : (hh + 1) * 256]
+                sc = jnp.where(far >= 0.0, sc - far * slopes[2 * hp + hh], NEG)
+                p.append(jnp.exp(sc - jnp.max(sc, axis=-1, keepdims=True)).astype(BF16))
+            values = jnp.concatenate([mqkv[8 + hp, rows, :], ones_256], axis=1)
+            o = dot(jnp.concatenate(p, axis=0), values)
+            o = o[:, :BLOCK] / o[:, BLOCK:]
+            attn[rows, pl.ds(pl.multiple_of(hp * BLOCK, BLOCK), BLOCK)] = jnp.where(
+                low_256, o[:256], o[256:]
+            ).astype(BF16)
 
     def out_copy(dz, dy, dl):
         tz, ty, tl = (zh + dz) % 2, (y + dy) % 4, (zl + dl) % 2

time: 58.4 us -> 57.3 us (0.981)
  Pallas kernels: 56.3 us -> 55.3 us
    pallas_call x1, Pallas kernels: 56.3 us -> 55.3 us  [per_device(): pl.pallas_call(kernel, out_shape=jax.ShapeDtypeStruct(weather.shape, BF16...]
where the time goes in v5:
time: 57.3 us; the launch traced here: 57.2 us
  Pallas kernels  55.3 us (97%)
  local copies, waits for them, and re-layouts  1.87 us (3%)
    pallas_call x1, Pallas kernels, per_device(): pl.pallas_call(kernel, out_shape=jax.ShapeDtypeStruct(weather.shape, BF16...  55.3 us
    unnamed x1, local copies, waits for them, and re-layouts  1.87 us

profile of v5, /device:TPU:1, one launch (start us, length us, event | category | flops | bytes accessed | tf_op | source)
XLA Modules:
  0.0 57.2 jit_solution(15264026590394237780)
XLA Ops:
  0.0 55.3 %axial.1 = bf16[2,2,128,512]{3,2,1,0:T(8,128)(2,1)} custom-call(bf16[2,2,128,512]{3,2,1,0:T(8,128)(2,1)} %weather.1, s32[2]{0:T(128)} %windows.1, s32[2,16]{1,0:T(2,128)} %table.1, f32[1,512]{1,0:T(1,128)} %bitcast.3, f32[1,512]{1,0:T(1,128)} %bitcast.4, f32[1,512]{1,0:T(1,128)} %bitcast.5, f32[8]{0:T(128)} %slopes.1, bf16[512,1536]{1,0:T(8,128)(2,1)} %lon_qkv_h.1, ...), custom_call_target="tpu_custom_call" | custom-call | tf_op jit(solution)/shard_map/axial/pallas_call | solution.py:384
  55.3 1.9 %copy.15 = bf16[2,2,128,512]{3,2,1,0:T(8,128)(2,1)} copy(bf16[2,2,128,512]{3,2,1,0:T(8,128)(2,1)} %axial.1) | data formatting | bytes 1048576

commit v6 on v5

--- a/solution.py
+++ b/solution.py
@@ -296,32 +296,9 @@
             for j in range(12):
                 mqkv[j, r0 : r0 + 64, :] = qkv[q * 64 : (q + 1) * 64, j * BLOCK : (j + 1) * BLOCK]
 
-    low_256 = lax.broadcasted_iota(jnp.int32, (256, BLOCK), 1) < 64
-    none = jnp.zeros((256, BLOCK), BF16)
+    low_128 = lax.broadcasted_iota(jnp.int32, (BLOCK, BLOCK), 1) < 64
+    none = jnp.zeros((BLOCK, BLOCK), BF16)
     ones_256 = jnp.ones((256, BLOCK), BF16)
-
-    @pl.loop(0, 4)
-    def _(hp):
-        far = dist[...]
-        scores = []
-        for g in range(2):
-            rows = slice(g * 256, (g + 1) * 256)
-            qp = mqkv[hp, rows, :] * jnp.bfloat16(0.125)
-            both = jnp.concatenate([jnp.where(low_256, qp, none), jnp.where(low_256, none, qp)], axis=0)
-            scores.append(dot_nt(both, mqkv[4 + hp, rows, :]))
-        for g in range(2):
-            rows = slice(g * 256, (g + 1) * 256)
-            p = []
-            for hh in range(2):
-                sc = scores[g][hh * 256 : (hh + 1) * 256]
-                sc = jnp.where(far >= 0.0, sc - far * slopes[2 * hp + hh], NEG)
-                p.append(jnp.exp(sc - jnp.max(sc, axis=-1, keepdims=True)).astype(BF16))
-            values = jnp.concatenate([mqkv[8 + hp, rows, :], ones_256], axis=1)
-            o = dot(jnp.concatenate(p, axis=0), values)
-            o = o[:, :BLOCK] / o[:, BLOCK:]
-            attn[rows, pl.ds(pl.multiple_of(hp * BLOCK, BLOCK), BLOCK)] = jnp.where(
-                low_256, o[:256], o[256:]
-            ).astype(BF16)
 
     def out_copy(dz, dy, dl):
         tz, ty, tl = (zh + dz) % 2, (y + dy) % 4, (zl + dl) % 2
@@ -337,6 +314,29 @@
         )
 
     for near in range(2):
+        @pl.loop(0, 4, step=4)
+        def _(hp0):
+            far = dist[near * 128 : near * 128 + 128, :]
+            units = [(hp0 + j, g) for j in range(4) for g in range(2)]
+            scores = []
+            for hp, g in units:
+                qp = mqkv[hp, g * 256 + near * 128 : g * 256 + near * 128 + 128, :] * jnp.bfloat16(0.125)
+                both = jnp.concatenate([jnp.where(low_128, qp, none), jnp.where(low_128, none, qp)], axis=0)
+                scores.append(dot_nt(both, mqkv[4 + hp, g * 256 : (g + 1) * 256, :]))
+            for (hp, g), both in zip(units, scores):
+                p = []
+                for hh in range(2):
+                    sc = both[hh * 128 : (hh + 1) * 128]
+                    sc = jnp.where(far >= 0.0, sc - far * slopes[2 * hp + hh], NEG)
+                    p.append(jnp.exp(sc - jnp.max(sc, axis=-1, keepdims=True)).astype(BF16))
+                values = jnp.concatenate([mqkv[8 + hp, g * 256 : (g + 1) * 256, :], ones_256], axis=1)
+                o = dot(jnp.concatenate(p, axis=0), values)
+                o = o[:, :BLOCK] / o[:, BLOCK:]
+                rows = slice(g * 256 + near * 128, g * 256 + near * 128 + 128)
+                attn[rows, pl.ds(pl.multiple_of(hp * BLOCK, BLOCK), BLOCK)] = jnp.where(
+                    low_128, o[:128], o[128:]
+                ).astype(BF16)
+
         halves = []
         for g in range(2):
             r0 = g * 256 + near * 128

time: 57.3 us -> 56.4 us (0.984)
  Pallas kernels: 55.3 us -> 54.3 us
    pallas_call x1, Pallas kernels: 55.3 us -> 54.3 us  [per_device(): pl.pallas_call(kernel, out_shape=jax.ShapeDtypeStruct(weather.shape, BF16...]
where the time goes in v6:
time: 56.4 us; the launch traced here: 56.2 us
  Pallas kernels  54.3 us (96%)
  local copies, waits for them, and re-layouts  1.87 us (3%)
    pallas_call x1, Pallas kernels, per_device(): pl.pallas_call(kernel, out_shape=jax.ShapeDtypeStruct(weather.shape, BF16...  54.3 us
    unnamed x1, local copies, waits for them, and re-layouts  1.87 us

profile of v6, /device:TPU:1, one launch (start us, length us, event | category | flops | bytes accessed | tf_op | source)
XLA Modules:
  0.0 56.2 jit_solution(2013506241180826267)
XLA Ops:
  0.0 54.3 %axial.1 = bf16[2,2,128,512]{3,2,1,0:T(8,128)(2,1)} custom-call(bf16[2,2,128,512]{3,2,1,0:T(8,128)(2,1)} %weather.1, s32[2]{0:T(128)} %windows.1, s32[2,16]{1,0:T(2,128)} %table.1, f32[1,512]{1,0:T(1,128)} %bitcast.3, f32[1,512]{1,0:T(1,128)} %bitcast.4, f32[1,512]{1,0:T(1,128)} %bitcast.5, f32[8]{0:T(128)} %slopes.1, bf16[512,1536]{1,0:T(8,128)(2,1)} %lon_qkv_h.1, ...), custom_call_target="tpu_custom_call" | custom-call | tf_op jit(solution)/shard_map/axial/pallas_call | solution.py:384
  54.3 1.9 %copy.15 = bf16[2,2,128,512]{3,2,1,0:T(8,128)(2,1)} copy(bf16[2,2,128,512]{3,2,1,0:T(8,128)(2,1)} %axial.1) | data formatting | bytes 1048576

commit v7 on v6

--- a/solution.py
+++ b/solution.py
@@ -206,10 +206,11 @@
                     o = dot(jnp.concatenate(p, axis=1), vaug[h, cells, :])
                     o = accum[h, rows, :] * jnp.exp(old - m) + o
                 if end:
-                    res.append(o / pltpu.roll(o, 64, 1))
+                    res.append(o)
                     if hh:
-                        attn[rows, pl.ds(pl.multiple_of(hp * BLOCK, BLOCK), BLOCK)] = jnp.where(
-                            low, res[-2], res[-1]
+                        attn[rows, pl.ds(pl.multiple_of(hp * BLOCK, BLOCK), BLOCK)] = (
+                            jnp.where(low, res[-2], res[-1])
+                            / pltpu.roll(jnp.where(low, res[-1], res[-2]), 64, 1)
                         ).astype(BF16)
                 else:
                     accum[h, rows, :] = o
@@ -331,10 +332,10 @@
                     p.append(jnp.exp(sc - jnp.max(sc, axis=-1, keepdims=True)).astype(BF16))
                 values = jnp.concatenate([mqkv[8 + hp, g * 256 : (g + 1) * 256, :], ones_256], axis=1)
                 o = dot(jnp.concatenate(p, axis=0), values)
-                o = o[:, :BLOCK] / o[:, BLOCK:]
+                total = jnp.where(low_128, o[:128, BLOCK:], o[128:, BLOCK:])
                 rows = slice(g * 256 + near * 128, g * 256 + near * 128 + 128)
-                attn[rows, pl.ds(pl.multiple_of(hp * BLOCK, BLOCK), BLOCK)] = jnp.where(
-                    low_128, o[:128], o[128:]
+                attn[rows, pl.ds(pl.multiple_of(hp * BLOCK, BLOCK), BLOCK)] = (
+                    jnp.where(low_128, o[:128, :BLOCK], o[128:, :BLOCK]) / total
                 ).astype(BF16)
 
         halves = []

time: 56.4 us -> 56.3 us (level)
  no operation moved by 1% of the time
where the time goes in v7:
time: 56.3 us; the launch traced here: 56.2 us
  Pallas kernels  54.3 us (96%)
  local copies, waits for them, and re-layouts  1.87 us (3%)
    pallas_call x1, Pallas kernels, per_device(): pl.pallas_call(kernel, out_shape=jax.ShapeDtypeStruct(weather.shape, BF16...  54.3 us
    unnamed x1, local copies, waits for them, and re-layouts  1.87 us

profile of v7, /device:TPU:1, one launch (start us, length us, event | category | flops | bytes accessed | tf_op | source)
XLA Modules:
  0.0 56.2 jit_solution(9385100550248156989)
XLA Ops:
  0.0 54.3 %axial.1 = bf16[2,2,128,512]{3,2,1,0:T(8,128)(2,1)} custom-call(bf16[2,2,128,512]{3,2,1,0:T(8,128)(2,1)} %weather.1, s32[2]{0:T(128)} %windows.1, s32[2,16]{1,0:T(2,128)} %table.1, f32[1,512]{1,0:T(1,128)} %bitcast.3, f32[1,512]{1,0:T(1,128)} %bitcast.4, f32[1,512]{1,0:T(1,128)} %bitcast.5, f32[8]{0:T(128)} %slopes.1, bf16[512,1536]{1,0:T(8,128)(2,1)} %lon_qkv_h.1, ...), custom_call_target="tpu_custom_call" | custom-call | tf_op jit(solution)/shard_map/axial/pallas_call | solution.py:385
  54.3 1.9 %copy.15 = bf16[2,2,128,512]{3,2,1,0:T(8,128)(2,1)} copy(bf16[2,2,128,512]{3,2,1,0:T(8,128)(2,1)} %axial.1) | data formatting | bytes 1048576
